TPU v7x, 32 devices: a whole 2x2x4 slice. The times are simulated.
32 devices in a mesh: dp: 4 (over y, x), seq: 8 (over z, core).
Axes of the slice: x: 2, y: 2, z: 4, core: 2. Of those that a mesh axis runs over, the one named last changes fastest.
Arguments:
- x_fwd: bfloat16 [16384, 1024], P(('dp', 'seq')), parts along dimension 0, may hold values from -6 to 6
- x_rev: bfloat16 [16384, 1024], P(('dp', 'seq')), parts along dimension 0, may hold values from -6 to 6
- gain: bfloat16 [1024], replicated, may hold values from 0.099609375 to 1.8984375
- w_qkv: bfloat16 [1024, 3072], replicated
Outputs:
- y_fwd: bfloat16 [16384, 1024], P(('dp', 'seq')), parts along dimension 0
- y_rev: bfloat16 [16384, 1024], P(('dp', 'seq')), parts along dimension 0
There are 4 independent parts, one for each index of `dp`. A program takes and returns all parts, laid end to end along the dimension named above; an argument that names none is the same for every part. Nothing has to cross between parts.
All inputs are finite; a program needn't handle non-finite values.
Results may differ from a plain program's by a relative error of at most 0.012.
Values may be sent and summed in bfloat16 or wider, within the bound.
A program may use at most 128 MiB of HBM per device.

v0:
```python
import jax
import jax.numpy as jnp
from jax import lax
from jax.sharding import PartitionSpec as P

HEADS = 16
WINDOW = 512


def extended_2(cells, sides, width):
    for axis, dim in sides:
        count = lax.axis_size(axis)
        ends = count - 1
        head = lax.slice_in_dim(cells, 0, width, axis=dim)
        tail = lax.slice_in_dim(cells, cells.shape[dim] - width, cells.shape[dim], axis=dim)
        cells = jnp.concatenate(
            [
                lax.ppermute(tail, axis, [(i, (i + 1) % count) for i in range(ends)]),
                cells,
                lax.ppermute(head, axis, [((i + 1) % count, i) for i in range(ends)]),
            ],
            axis=dim,
        )
    return cells


def attend(stacked, gain, w_qkv):
    rows = stacked.shape[1]
    width = stacked.shape[2]
    head_size = width // HEADS
    per_group = 2
    group_width = per_group * head_size
    span = rows + 2 * WINDOW
    scale = head_size ** (-0.5)
    xf = stacked.astype(jnp.float32)
    meansq = jnp.mean(xf * xf, axis=-1, keepdims=True)
    normed = (xf * lax.rsqrt(meansq + 1e-06) * gain.astype(jnp.float32)).astype(jnp.bfloat16)
    qkv = jnp.dot(normed.reshape(2 * rows, width), w_qkv, preferred_element_type=jnp.float32)
    qkv = qkv.astype(jnp.bfloat16).reshape(2, rows, 3 * width)
    query = qkv[:, :, :width]
    keyval = qkv[:, :, width:]
    extended = extended_2(keyval, (("seq", 1),), WINDOW)
    length = rows * lax.axis_size("seq")
    start = lax.axis_index("seq") * rows
    qpos = start + jnp.arange(rows, dtype=jnp.int32)
    kpos = start - WINDOW + jnp.arange(span, dtype=jnp.int32)
    inside = (
        (jnp.abs(qpos[:, None] - kpos[None, :]) <= WINDOW)
        & (kpos[None, :] >= 0)
        & (kpos[None, :] < length)
    )

    def group_heads(group):
        offset = group * group_width
        qgroup = lax.dynamic_slice_in_dim(query, offset, group_width, 2).reshape(
            2, rows, per_group, head_size
        )
        kgroup = lax.dynamic_slice_in_dim(extended, offset, group_width, 2).reshape(
            2, span, per_group, head_size
        )
        vgroup = lax.dynamic_slice_in_dim(extended, width + offset, group_width, 2).reshape(
            2, span, per_group, head_size
        )
        scores = (
            jnp.einsum("srhd,skhd->shrk", qgroup, kgroup, preferred_element_type=jnp.float32)
            * scale
        )
        scores = jnp.where(inside[None, None], scores, -1e30)
        top = jnp.max(scores, axis=-1, keepdims=True)
        probs = jnp.exp(scores - top)
        denom = jnp.sum(probs, axis=-1)
        weights = probs.astype(jnp.bfloat16)
        out = jnp.einsum("shrk,skhd->srhd", weights, vgroup, preferred_element_type=jnp.float32)
        out = out / jnp.transpose(denom, (0, 2, 1))[:, :, :, None]
        return out.reshape(2, rows, group_width).astype(jnp.bfloat16)

    grouped = lax.map(group_heads, jnp.arange(HEADS // per_group, dtype=jnp.int32))
    return jnp.transpose(grouped, (1, 2, 0, 3)).reshape(2, rows, width)


def split_pieces(block):
    count = lax.axis_size("seq")
    lead = block.shape[0]
    rows = block.shape[1]
    width = block.shape[2]
    return block.reshape(lead, rows, count, width // count)


def combine_outputs(attended, moved):
    partner = moved[:, ::-1, ::-1].astype(jnp.float32)
    near = attended.astype(jnp.float32)
    y_fwd = (near[0] + partner[1]).astype(jnp.bfloat16)
    y_rev = (near[1] + partner[0]).astype(jnp.bfloat16)
    return (y_fwd, y_rev)


def per_device(x_fwd, x_rev, gain, w_qkv):
    attended = attend(jnp.stack([x_fwd, x_rev]), gain, w_qkv)
    pieces = split_pieces(attended)
    spread = lax.all_to_all(pieces, "seq", split_axis=2, concat_axis=2, tiled=True)[:, :, ::-1]
    moved = lax.all_to_all(spread, "seq", split_axis=2, concat_axis=2, tiled=True).reshape(
        attended.shape
    )
    y_fwd, y_rev = combine_outputs(attended, moved)
    return (y_fwd, y_rev)


def solution(mesh):
    in_specs = (P(("dp", "seq"), None), P(("dp", "seq"), None), P(), P())
    out_specs = (P(("dp", "seq"), None), P(("dp", "seq"), None))
    return jax.shard_map(
        per_device, mesh=mesh, in_specs=in_specs, out_specs=out_specs, check_vma=False
    )
```

profile of v0, /device:TPU:0, one launch (start us, length us, event | category | flops | bytes accessed | tf_op | source)
XLA Modules:
  0.0 363.7 jit_solution(14860233346022252226)
XLA Ops:
  0.7 2.0 maximum_convert_fusion
  4.9 7.1 %convolution_convert_fusion = bf16[1024,3072]{1,0:T(8,128)(2,1)S(1)} fusion(bf16[1024,1024]{1,0:T(8,128)(2,1)S(1)} %fusion.22, bf16[1024,3072]{1,0:T(8,128)(2,1)S(1)} %bitcast.75), kind=kOutput, calls=%fused_computation.21 | convolution fusion | flops 6445596672 | bytes 14680064 | tf_op jit(solution)/shard_map/dot_general | solution.py:38
  12.0 2.6 copy-done.2
  14.7 2.3 slice.32
  17.0 6.3 %copy.13 = bf16[2,512,2048]{1,2,0:T(8,128)(2,1)} copy(bf16[2,512,2048]{2,1,0:T(8,128)(2,1)} %slice.32) | data formatting | bytes 8388608
  23.3 4.3 %collective-permute-start = (bf16[2,512,2048]{1,2,0:T(8,128)(2,1)}, bf16[2,512,2048]{1,2,0:T(8,128)(2,1)}, u32[]{:S(2)}, u32[]{:S(2)}) collective-permute-start(bf16[2,512,2048]{1,2,0:T(8,128)(2,1)} %copy.13), channel_id=1, source_target_pairs={{0,1},{1,2},{2,3},{3,4},{4,5},{5,6},{6,7},{8,9},{9,10},{10,11},{11... | collective-permute-start | bytes 12582920 | tf_op jit(solution)/shard_map/ppermute | solution.py:18
  28.9 3.1 slice.33
  32.7 4.5 %collective-permute-done.1 = bf16[2,512,2048]{1,2,0:T(8,128)(2,1)} collective-permute-done((bf16[2,512,2048]{1,2,0:T(8,128)(2,1)}, bf16[2,512,2048]{1,2,0:T(8,128)(2,1)}, u32[]{:S(2)}, u32[]{:S(2)}) %collective-permute-start.1) | collective-permute-done | bytes 4194336 | tf_op jit(solution)/shard_map/ppermute | solution.py:20
  37.2 10.3 %pad_maximum_fusion = bf16[2,1536,2048]{1,2,0:T(8,128)(2,1)} fusion(bf16[2,512,2048]{1,2,0:T(8,128)(2,1)} %collective-permute-done.1, bf16[2,512,2048]{1,2,0:T(8,128)(2,1)} %copy.13, bf16[2,512,2048]{1,2,0:T(8,128)(2,1)} %collective-permute-done), kind=kLoop, calls=%fused_computation.20 | loop fusion | flops 37748736 | bytes 25165824 | tf_op jit(solution)/shard_map/concatenate | solution.py:16
  47.5 120.5 %while.13 = (s32[]{:T(128)}, bf16[8,2,512,128]{2,3,1,0:T(8,128)(2,1)}, s32[8]{0:T(128)S(1)}, bf16[2,1536,2048]{1,2,0:T(8,128)(2,1)}, bf16[2,512,1024]{2,1,0:T(8,...) while((s32[]{:T(128)}, ...), condition=%wide.region_4.5_spmd.clone, body=%wide.region_1.4_spmd.clone.sunk | while | flops 844099584 | bytes 47763212 | solution.py:77
  48.8 1.5 constant_dynamic-slice_fusion.5
  52.5 2.5 fusion.48
  55.0 3.5 fusion.49
  58.5 3.3 fusion.50
  67.6 2.5 fusion.48
  70.1 3.5 fusion.49
  73.6 3.3 fusion.50
  78.9 1.5 constant_dynamic-slice_fusion.5
  82.6 2.5 fusion.48
  85.1 3.5 fusion.49
  88.7 3.3 fusion.50
  97.7 2.5 fusion.48
  100.2 3.5 fusion.49
  103.7 3.3 fusion.50
  112.8 2.5 fusion.48
  115.3 3.5 fusion.49
  118.8 3.3 fusion.50
  127.8 2.5 fusion.48
  130.3 3.5 fusion.49
  133.8 3.3 fusion.50
  142.9 2.5 fusion.48
  145.4 3.5 fusion.49
  148.9 3.3 fusion.50
  157.9 2.5 fusion.48
  160.4 3.5 fusion.49
  164.0 3.3 fusion.50
  168.0 94.2 %all_to_all.10 = bf16[2,512,8,128]{1,3,0,2:T(8,128)(2,1)} all-to-all(bf16[2,512,8,128]{1,3,0,2:T(8,128)(2,1)} %bitcast.61), channel_id=1, replica_groups=mesh['dp'=4,'seq'=8] {'seq'}, dimensions={2} | all-to-all | bytes 4194304 | tf_op jit(solution)/shard_map/all_to_all | solution.py:100
  262.3 3.3 rev.6
  265.5 4.5 %all-to-all-start.1 = ((bf16[2,512,8,128]{1,3,0,2:T(8,128)(2,1)}), bf16[2,512,8,128]{1,3,0,2:T(8,128)(2,1)}, u32[]{:S(2)}, u32[]{:S(2)}) async-start(bf16[2,512,8,128]{1,3,0,2:T(8,128)(2,1)} %rev.6), calls=%async_computation.1 | async-start | bytes 4194304 | tf_op jit(solution)/shard_map/all_to_all | solution.py:101
  270.6 2.7 fusion.29
  273.3 1.9 copy.11
  275.3 2.9 copy.12
  278.2 40.8 %all-to-all-done.1 = bf16[2,512,8,128]{1,3,0,2:T(8,128)(2,1)} async-done(((bf16[2,512,8,128]{1,3,0,2:T(8,128)(2,1)}), bf16[2,512,8,128]{1,3,0,2:T(8,128)(2,1)}, u32[]{:S(2)}, u32[]{:S(2)}) %all-to-all-start.1) | async-done | bytes 2097184 | tf_op jit(solution)/shard_map/all_to_all | solution.py:101
  318.9 4.3 %copy.9 = bf16[2,512,8,128]{3,2,1,0:T(8,128)(2,1)} copy(bf16[2,512,8,128]{1,3,0,2:T(8,128)(2,1)} %all-to-all-done.1) | data formatting | bytes 4194304 | tf_op jit(solution)/shard_map/all_to_all | solution.py:101
  323.2 4.2 %reshape.94 = bf16[2,512,1024]{2,1,0:T(8,128)(2,1)} reshape(bf16[2,512,8,128]{3,2,1,0:T(8,128)(2,1)} %copy.9) | data formatting | bytes 4194304 | tf_op jit(solution)/shard_map/reshape | solution.py:101
  327.4 32.1 %rev.7 = bf16[2,512,1024]{2,1,0:T(8,128)(2,1)} reverse(bf16[2,512,1024]{2,1,0:T(8,128)(2,1)} %reshape.94), dimensions={1,2} | reverse | bytes 4194304 | tf_op jit(solution)/shard_map/rev | solution.py:90
  359.5 2.2 convert_element_type.67
  361.7 2.0 fusion.26
  (75 shorter events, 42.1 us)
Async XLA Ops:
  0.6 2.0 copy-start.4
  0.6 2.2 copy-start.3
  0.6 2.7 copy-start.5
  0.7 3.5 slice-start
  2.8 2.1 slice-start.1
  12.0 2.7 copy-start.2
  23.3 9.5 %collective-permute-start = (bf16[2,512,2048]{1,2,0:T(8,128)(2,1)}, bf16[2,512,2048]{1,2,0:T(8,128)(2,1)}, u32[]{:S(2)}, u32[]{:S(2)}) collective-permute-start(bf16[2,512,2048]{1,2,0:T(8,128)(2,1)} %copy.13), channel_id=1, source_target_pairs={{0,1},{1,2},{2,3},{3,4},{4,5},{5,6},{6,7},{8,9},{9,10},{10,11},{11... | collective-permute-start | bytes 12582920 | tf_op jit(solution)/shard_map/ppermute | solution.py:18
  27.6 9.6 %collective-permute-start.1 = (bf16[2,512,2048]{1,2,0:T(8,128)(2,1)}, bf16[2,512,2048]{1,2,0:T(8,128)(2,1)}, u32[]{:S(2)}, u32[]{:S(2)}) collective-permute-start(bf16[2,512,2048]{1,2,0:T(8,128)(2,1)} %copy.13), channel_id=1, source_target_pairs={{1,0},{2,1},{3,2},{4,3},{5,4},{6,5},{7,6},{9,8},{10,9},{11,10},{12... | collective-permute-start | bytes 12582920 | tf_op jit(solution)/shard_map/ppermute | solution.py:20
  262.3 7.8 %copy-start = (bf16[8,2,512,128]{2,3,1,0:T(8,128)(2,1)S(1)}, bf16[8,2,512,128]{2,3,1,0:T(8,128)(2,1)}, u32[]{:S(2)}) copy-start(bf16[8,2,512,128]{2,3,1,0:T(8,128)(2,1)} %get-tuple-element.79) | copy-start | bytes 6291460
  265.5 53.4 %all-to-all-start.1 = ((bf16[2,512,8,128]{1,3,0,2:T(8,128)(2,1)}), bf16[2,512,8,128]{1,3,0,2:T(8,128)(2,1)}, u32[]{:S(2)}, u32[]{:S(2)}) async-start(bf16[2,512,8,128]{1,3,0,2:T(8,128)(2,1)} %rev.6), calls=%async_computation.1 | async-start | bytes 4194304 | tf_op jit(solution)/shard_map/all_to_all | solution.py:101
  359.5 2.2 copy-start.1
where the time goes:
time: 369 us; the launch traced here: 364 us
  local copies, waits for them, and re-layouts  98.4 us (27%)
  blocking collectives  94.2 us (26%)
  other arithmetic  55 us (15%)
  matrix products  53.6 us (15%)
  waiting for transfers between devices  45.9 us (12%)
  starting transfers between devices  10.1 us (3%)
  loops' own time  5.67 us (2%)
    all_to_all x1, blocking collectives, per_device(): lax.all_to_all(pieces, 'seq', split_axis=2, concat_axis=2, tiled=True)  94.2 us
    all_to_all x1, waiting for transfers between devices, per_device(): lax.all_to_all(spread, 'seq', split_axis=2, concat_axis=2, tiled=True)  40.8 us
    rev x1, local copies, waits for them, and re-layouts, combine_outputs(): partner = moved[:, ::-1, ::-1].astype(jnp.float32)  32.1 us
    reduce_sum x8, other arithmetic, group_heads(): denom = jnp.sum(probs, axis=-1)  28.1 us
    dot_general x8, matrix products, group_heads(): jnp.einsum('shrk,skhd->srhd', weights, vgroup, preferred_element_type=jnp...  26.5 us
    dot_general x8, matrix products, group_heads(): jnp.einsum('srhd,skhd->shrk', qgroup, kgroup, preferred_element_type=jnp....  20 us
    dynamic_slice x8, local copies, waits for them, and re-layouts, group_heads(): lax.dynamic_slice_in_dim(extended, offset, group_width, 2)  11.9 us
    unnamed x18, local copies, waits for them, and re-layouts  10.3 us
  transfers between devices with their start and end apart: 3, of which 3 were waited for; matrix products, arithmetic and copies ran while one was open for 3% of the time, Pallas kernels for 0%

commit v1 on v0

v1 whole, which is shorter than its diff:
```python
import functools
import math

import jax
import jax.numpy as jnp
from jax import lax
from jax.experimental import pallas as pl
from jax.experimental.pallas import tpu as pltpu
from jax.sharding import PartitionSpec as P

HEADS = 16
WINDOW = 512
BLOCK = 256
TILE = 512
LANES = 128
GROUPS = 4
VMEM_LIMIT = 48 * 1024 * 1024


def project_kernel(parts, gain_ref, *refs):
    x_refs = refs[:parts]
    w_ref, out_ref, hn_ref = refs[parts:]
    rows = x_refs[0].shape[0]

    @pl.when(pl.program_id(0) == 0)
    def _():
        gain = gain_ref[...].astype(jnp.float32)
        for part in range(parts):
            for start in range(0, rows, BLOCK):
                xf = x_refs[part][start:start + BLOCK, :].astype(jnp.float32)
                meansq = jnp.mean(xf * xf, axis=-1, keepdims=True)
                hn = xf * lax.rsqrt(meansq + 1e-06) * gain
                hn_ref[part * rows + start:part * rows + start + BLOCK, :] = hn.astype(jnp.bfloat16)

    out_ref[...] = jnp.dot(
        hn_ref[...], w_ref[...], preferred_element_type=jnp.float32
    ).astype(jnp.bfloat16)


def project(xs, gain, w, first_col):
    rows, width = xs[0].shape
    cols = w.shape[1] - first_col
    total = rows * len(xs)
    return pl.pallas_call(
        functools.partial(project_kernel, len(xs)),
        grid=(cols // TILE,),
        in_specs=[pl.BlockSpec((1, width), lambda j: (0, 0))]
        + [pl.BlockSpec((rows, width), lambda j: (0, 0)) for _ in xs]
        + [pl.BlockSpec((width, TILE), lambda j: (0, j + first_col // TILE))],
        out_specs=pl.BlockSpec((total, TILE), lambda j: (0, j)),
        out_shape=jax.ShapeDtypeStruct((total, cols), jnp.bfloat16),
        scratch_shapes=[pltpu.VMEM((total, width), jnp.bfloat16)],
        compiler_params=pltpu.CompilerParams(vmem_limit_bytes=VMEM_LIMIT),
        cost_estimate=pl.CostEstimate(
            flops=2 * total * width * cols,
            bytes_accessed=2 * (total * width + width * cols + total * cols),
            transcendentals=0,
        ),
    )(gain, *xs, w)


def attend_kernel(scale, bias_ref, flip_ref, q_ref, kl, ko, kr, vl, vo, vr, o_ref, mirror_ref, kx, vx):
    rows = q_ref.shape[0]
    span = 2 * WINDOW + BLOCK
    blocks = rows // BLOCK
    kx[:WINDOW, :] = kl[...]
    kx[WINDOW:WINDOW + rows, :] = ko[...]
    kx[WINDOW + rows:, :] = kr[...]
    start = 0
    for ref in (vl, vo, vr):
        v = ref[...]
        low = lax.broadcasted_iota(jnp.int32, v.shape, 1) < LANES // 2
        one = jnp.ones_like(v)
        vx[0, start:start + v.shape[0], :] = jnp.where(low, v, one)
        vx[1, start:start + v.shape[0], :] = jnp.where(low, one, v)
        start += v.shape[0]
    low = lax.broadcasted_iota(jnp.int32, (BLOCK, LANES), 1) < LANES // 2
    flip = flip_ref[...]
    for block in range(blocks):
        q = q_ref[block * BLOCK:(block + 1) * BLOCK, :]
        keys = kx[block * BLOCK:block * BLOCK + span, :]
        bias = bias_ref[block]
        outs = []
        for head in range(2):
            qh = jnp.where(low if head == 0 else ~low, q, jnp.zeros_like(q))
            s = lax.dot_general(
                qh, keys, (((1,), (1,)), ((), ())), preferred_element_type=jnp.float32
            )
            s = s * scale + bias
            top = jnp.max(s, axis=-1, keepdims=True)
            p = jnp.exp2(s - top).astype(jnp.bfloat16)
            outs.append(
                jnp.dot(
                    p,
                    vx[head, block * BLOCK:block * BLOCK + span, :],
                    preferred_element_type=jnp.float32,
                )
            )
        num = jnp.where(low, outs[0], outs[1])
        den = pltpu.roll(jnp.where(low, outs[1], outs[0]), LANES // 2, 1)
        a = (num / den).astype(jnp.bfloat16)
        o_ref[block * BLOCK:(block + 1) * BLOCK, :] = a
        turned = jnp.dot(flip, a, preferred_element_type=jnp.float32).astype(jnp.bfloat16)
        turned = jnp.dot(
            turned, flip[:LANES, BLOCK - LANES:], preferred_element_type=jnp.float32
        ).astype(jnp.bfloat16)
        other = blocks - 1 - block
        mirror_ref[other * BLOCK:(other + 1) * BLOCK, :] = turned


def attend(bias, flip, own, halo, group):
    rows = own.shape[0]
    width = own.shape[1] // 3
    pairs = width // LANES // GROUPS
    first = group * pairs
    per = width // LANES
    head_size = width // HEADS
    span = 2 * WINDOW + BLOCK
    blocks = rows // BLOCK
    scale = head_size ** (-0.5) * math.log2(math.e)

    def part(size, row, offset):
        return pl.BlockSpec((size, LANES), lambda j: (row, j + first + offset))

    return pl.pallas_call(
        functools.partial(attend_kernel, scale),
        grid=(pairs,),
        in_specs=[
            pl.BlockSpec(bias.shape, lambda j: (0, 0, 0)),
            pl.BlockSpec(flip.shape, lambda j: (0, 0)),
            part(rows, 0, 0),
            part(WINDOW, 0, 0),
            part(rows, 0, per),
            part(WINDOW, 1, 0),
            part(WINDOW, 0, per),
            part(rows, 0, 2 * per),
            part(WINDOW, 1, per),
        ],
        out_specs=[
            pl.BlockSpec((rows, LANES), lambda j: (0, j)),
            pl.BlockSpec((rows, LANES), lambda j: (0, pairs - 1 - j)),
        ],
        out_shape=[jax.ShapeDtypeStruct((rows, pairs * LANES), jnp.bfloat16)] * 2,
        scratch_shapes=[
            pltpu.VMEM((rows + 2 * WINDOW, LANES), jnp.bfloat16),
            pltpu.VMEM((2, rows + 2 * WINDOW, LANES), jnp.bfloat16),
        ],
        compiler_params=pltpu.CompilerParams(vmem_limit_bytes=VMEM_LIMIT),
        cost_estimate=pl.CostEstimate(
            flops=pairs * blocks * 8 * 2 * BLOCK * span * LANES,
            bytes_accessed=2 * pairs * LANES * (6 * rows + 4 * WINDOW) + bias.size * 4,
            transcendentals=pairs * 2 * rows * span,
        ),
    )(bias, flip, own, halo, own, halo, halo, own, halo)


def band(rows):
    span = 2 * WINDOW + BLOCK
    index = lax.axis_index("seq")
    low = jnp.where(index == 0, WINDOW, 0)
    high = jnp.where(index == lax.axis_size("seq") - 1, WINDOW + rows, 2 * WINDOW + rows)
    shape = (rows // BLOCK, BLOCK, span)
    base = lax.broadcasted_iota(jnp.int32, shape, 0) * BLOCK
    query = lax.broadcasted_iota(jnp.int32, shape, 1)
    key = lax.broadcasted_iota(jnp.int32, shape, 2)
    inside = (key >= query) & (key <= query + 2 * WINDOW) & (key + base >= low) & (key + base < high)
    return jnp.where(inside, 0.0, -1e30).astype(jnp.float32)


def per_device(x_fwd, x_rev, gain, w_qkv):
    rows = x_fwd.shape[0]
    count = lax.axis_size("seq")
    up = [(i, i + 1) for i in range(count - 1)]
    down = [(i + 1, i) for i in range(count - 1)]
    mirror = [(i, count - 1 - i) for i in range(count)]
    gain = gain.reshape(1, -1)

    halos = []
    for x in (x_fwd, x_rev):
        left = lax.ppermute(x[rows - WINDOW:], "seq", up)
        right = lax.ppermute(x[:WINDOW], "seq", down)
        halos.append((left, right))
    bias = band(rows)
    flip = jnp.flip(jnp.eye(BLOCK, dtype=jnp.bfloat16), axis=0)
    owns = [project((x,), gain, w_qkv, 0) for x in (x_fwd, x_rev)]
    near, far = [], []
    for strand in range(2):
        halo = project(halos[strand], gain, w_qkv, x_fwd.shape[1])
        for group in range(GROUPS):
            a, turned = attend(bias, flip, owns[strand], halo, group)
            near.append(a.astype(jnp.float32))
            far.append(lax.ppermute(turned, "seq", mirror).astype(jnp.float32))
    outs = []
    for strand in range(2):
        outs.append(
            jnp.concatenate(
                [
                    (near[strand * GROUPS + g] + far[(1 - strand) * GROUPS + GROUPS - 1 - g]).astype(jnp.bfloat16)
                    for g in range(GROUPS)
                ],
                axis=1,
            )
        )
    return tuple(outs)


def solution(mesh):
    in_specs = (P(("dp", "seq"), None), P(("dp", "seq"), None), P(), P())
    out_specs = (P(("dp", "seq"), None), P(("dp", "seq"), None))
    return jax.shard_map(
        per_device, mesh=mesh, in_specs=in_specs, out_specs=out_specs, check_vma=False
    )
```

time: 369 us -> 195 us (0.53)
  the two profiles are of different devices: /device:TPU:0 before, /device:TPU:12 now
where the time goes in v1:
time: 195 us; the launch traced here: 193 us
  Pallas kernels  98.6 us (51%)
  waiting for transfers between devices  64.8 us (33%)
  starting transfers between devices  19.9 us (10%)
  local copies, waits for them, and re-layouts  5.51 us (3%)
  other arithmetic  3.35 us (2%)
    pallas_call x8, Pallas kernels, attend(): pl.pallas_call(functools.partial(attend_kernel, scale), grid=(pairs,), in...  66.5 us
    ppermute x8, waiting for transfers between devices, per_device(): far.append(lax.ppermute(turned, 'seq', mirror).astype(jnp.float32))  64.8 us
    pallas_call x4, Pallas kernels, project(): pl.pallas_call(functools.partial(project_kernel, len(xs)), grid=(cols //...  32.2 us
    ppermute x8, starting transfers between devices, per_device(): far.append(lax.ppermute(turned, 'seq', mirror).astype(jnp.float32))  10.5 us
    ppermute x2, starting transfers between devices, per_device(): right = lax.ppermute(x[:WINDOW], 'seq', down)  5.08 us
    unnamed x8, local copies, waits for them, and re-layouts  4.65 us
    ppermute x2, starting transfers between devices, per_device(): left = lax.ppermute(x[rows - WINDOW:], 'seq', up)  4.33 us
  transfers between devices with their start and end apart: 12, of which 5 were waited for; matrix products, arithmetic and copies ran while one was open for 2% of the time, Pallas kernels for 38%

profile of v1, /device:TPU:12, one launch (start us, length us, event | category | flops | bytes accessed | tf_op | source)
XLA Modules:
  0.0 193.1 jit_solution(6014857948189053397)
XLA Ops:
  0.6 1.9 collective-permute-start.1
  2.6 2.4 %collective-permute-start = (bf16[512,1024]{1,0:T(8,128)(2,1)}, bf16[512,1024]{1,0:T(8,128)(2,1)S(1)}, u32[]{:S(2)}, u32[]{:S(2)}) collective-permute-start(bf16[512,1024]{1,0:T(8,128)(2,1)} %refs_0_.2), channel_id=1, source_target_pairs={{0,1},{1,2},{2,3},{3,4},{4,5},{5,6},{6,7},{8,9},{9,10},{10,11},{11... | collective-permute-start | bytes 3145736 | tf_op jit(solution)/shard_map/ppermute | solution.py:180
  5.0 3.2 %collective-permute-start.3 = (bf16[512,1024]{1,0:T(8,128)(2,1)}, bf16[512,1024]{1,0:T(8,128)(2,1)}, u32[]{:S(2)}, u32[]{:S(2)}) collective-permute-start(bf16[512,1024]{1,0:T(8,128)(2,1)} %refs_0_.3), channel_id=1, source_target_pairs={{1,0},{2,1},{3,2},{4,3},{5,4},{6,5},{7,6},{9,8},{10,9},{11,10},{12... | collective-permute-start | bytes 3145736 | tf_op jit(solution)/shard_map/ppermute | solution.py:181
  8.1 1.9 collective-permute-start.2
  10.1 0.7 reshape.7.gain_ref
  10.8 0.2 rev.4.flip_ref
  11.0 0.0 copy-start.2
  11.0 1.2 copy-done.2
  12.2 7.3 %shard_map.62.q_ref.ko.vo = bf16[512,3072]{1,0:T(8,128)(2,1)S(1)} custom-call(bf16[1,1024]{1,0:T(2,128)(2,1)S(1)} %reshape.7.gain_ref, bf16[512,1024]{1,0:T(8,128)(2,1)S(1)} %copy-done.2, bf16[1024,3072]{1,0:T(8,128)(2,1)} %refs_2_.3), custom_call_target="tpu_custom_call" | custom-call | flops 3221225472 | bytes 10485760 | tf_op jit(solution)/shard_map/pallas_call | solution.py:44
  19.5 1.7 copy-done.1
  21.3 7.2 %shard_map.59.q_ref.ko.vo = bf16[512,3072]{1,0:T(8,128)(2,1)S(1)} custom-call(bf16[1,1024]{1,0:T(2,128)(2,1)S(1)} %reshape.7.gain_ref, bf16[512,1024]{1,0:T(8,128)(2,1)S(1)} %copy-done.3, bf16[1024,3072]{1,0:T(8,128)(2,1)} %refs_2_.3), custom_call_target="tpu_custom_call" | custom-call | flops 3221225472 | bytes 10485760 | tf_op jit(solution)/shard_map/pallas_call | solution.py:44
  28.5 1.7 copy-done
  30.2 0.6 fusion.4.bias_ref
  30.7 0.0 collective-permute-done.2.refs_0_
  30.8 9.2 %shard_map.63.kl.kr.vl.vr = bf16[1024,2048]{1,0:T(8,128)(2,1)} custom-call(bf16[1,1024]{1,0:T(2,128)(2,1)S(1)} %reshape.7.gain_ref, bf16[512,1024]{1,0:T(8,128)(2,1)} %collective-permute-done.2.refs_0_, bf16[512,1024]{1,0:T(8,128)(2,1)} %collective-permute-done.3.refs_1_, bf16[1024,3072]{1,0:T(8,128)(2,1)} %refs_2_.3), custom_call_target="tpu_custom_call" | custom-call | flops 4294967296 | bytes 10485760 | tf_op jit(solution)/shard_map/pallas_call | solution.py:44
  39.9 8.2 %shard_map.70 = (bf16[512,256]{1,0:T(8,128)(2,1)S(1)}, bf16[512,256]{1,0:T(8,128)(2,1)S(1)}) custom-call(f32[2,256,1280]{2,1,0:T(8,128)S(1)} %fusion.4.bias_ref, bf16[256,256]{1,0:T(8,128)(2,1)S(1)} %rev.4.flip_ref, bf16[512,3072]{1,0:T(8,128)(2,1)} %copy-done.1, bf16[1024,2048]{1,0:T(8,128)(2,1)} %shard_map.63.kl.kr.vl.vr, bf16[512,3072]{1,0:T(8,128)(2,1)} %copy-done.1, ...), custom_call_target="tpu_custom_call" | custom-call | flops 2684354560 | bytes 5242880 | tf_op jit(solution)/shard_map/pallas_call | solution.py:125
  48.2 8.3 %shard_map.68 = (bf16[512,256]{1,0:T(8,128)(2,1)S(1)}, bf16[512,256]{1,0:T(8,128)(2,1)S(1)}) custom-call(f32[2,256,1280]{2,1,0:T(8,128)S(1)} %fusion.4.bias_ref, bf16[256,256]{1,0:T(8,128)(2,1)S(1)} %rev.4.flip_ref, bf16[512,3072]{1,0:T(8,128)(2,1)} %copy-done.1, bf16[1024,2048]{1,0:T(8,128)(2,1)} %shard_map.63.kl.kr.vl.vr, bf16[512,3072]{1,0:T(8,128)(2,1)} %copy-done.1, ...), custom_call_target="tpu_custom_call" | custom-call | flops 2684354560 | bytes 5242880 | tf_op jit(solution)/shard_map/pallas_call | solution.py:125
  56.5 8.5 %shard_map.66 = (bf16[512,256]{1,0:T(8,128)(2,1)S(1)}, bf16[512,256]{1,0:T(8,128)(2,1)S(1)}) custom-call(f32[2,256,1280]{2,1,0:T(8,128)S(1)} %fusion.4.bias_ref, bf16[256,256]{1,0:T(8,128)(2,1)S(1)} %rev.4.flip_ref, bf16[512,3072]{1,0:T(8,128)(2,1)} %copy-done.1, bf16[1024,2048]{1,0:T(8,128)(2,1)} %shard_map.63.kl.kr.vl.vr, bf16[512,3072]{1,0:T(8,128)(2,1)} %copy-done.1, ...), custom_call_target="tpu_custom_call" | custom-call | flops 2684354560 | bytes 5242880 | tf_op jit(solution)/shard_map/pallas_call | solution.py:125
  64.9 8.3 %shard_map.64 = (bf16[512,256]{1,0:T(8,128)(2,1)S(1)}, bf16[512,256]{1,0:T(8,128)(2,1)S(1)}) custom-call(f32[2,256,1280]{2,1,0:T(8,128)S(1)} %fusion.4.bias_ref, bf16[256,256]{1,0:T(8,128)(2,1)S(1)} %rev.4.flip_ref, bf16[512,3072]{1,0:T(8,128)(2,1)} %copy-done.1, bf16[1024,2048]{1,0:T(8,128)(2,1)} %shard_map.63.kl.kr.vl.vr, bf16[512,3072]{1,0:T(8,128)(2,1)} %copy-done.1, ...), custom_call_target="tpu_custom_call" | custom-call | flops 2684354560 | bytes 5242880 | tf_op jit(solution)/shard_map/pallas_call | solution.py:125
  73.2 0.0 collective-permute-done.refs_0_
  73.2 8.5 %shard_map.60.kl.kr.vl.vr = bf16[1024,2048]{1,0:T(8,128)(2,1)} custom-call(bf16[1,1024]{1,0:T(2,128)(2,1)S(1)} %reshape.7.gain_ref, bf16[512,1024]{1,0:T(8,128)(2,1)S(1)} %collective-permute-done.refs_0_, bf16[512,1024]{1,0:T(8,128)(2,1)S(1)} %collective-permute-done.1.refs_1_, bf16[1024,3072]{1,0:T(8,128)(2,1)} %refs_2_.3), custom_call_target="tpu_custom_call" | custom-call | flops 4294967296 | bytes 10485760 | tf_op jit(solution)/shard_map/pallas_call | solution.py:44
  81.7 8.3 %shard_map.69 = (bf16[512,256]{1,0:T(8,128)(2,1)S(1)}, bf16[512,256]{1,0:T(8,128)(2,1)S(1)}) custom-call(f32[2,256,1280]{2,1,0:T(8,128)S(1)} %fusion.4.bias_ref, bf16[256,256]{1,0:T(8,128)(2,1)S(1)} %rev.4.flip_ref, bf16[512,3072]{1,0:T(8,128)(2,1)} %copy-done, bf16[1024,2048]{1,0:T(8,128)(2,1)} %shard_map.60.kl.kr.vl.vr, bf16[512,3072]{1,0:T(8,128)(2,1)} %copy-done, ...), custom_call_target="tpu_custom_call" | custom-call | flops 2684354560 | bytes 5242880 | tf_op jit(solution)/shard_map/pallas_call | solution.py:125
  90.0 8.5 %shard_map.67 = (bf16[512,256]{1,0:T(8,128)(2,1)S(1)}, bf16[512,256]{1,0:T(8,128)(2,1)S(1)}) custom-call(f32[2,256,1280]{2,1,0:T(8,128)S(1)} %fusion.4.bias_ref, bf16[256,256]{1,0:T(8,128)(2,1)S(1)} %rev.4.flip_ref, bf16[512,3072]{1,0:T(8,128)(2,1)} %copy-done, bf16[1024,2048]{1,0:T(8,128)(2,1)} %shard_map.60.kl.kr.vl.vr, bf16[512,3072]{1,0:T(8,128)(2,1)} %copy-done, ...), custom_call_target="tpu_custom_call" | custom-call | flops 2684354560 | bytes 5242880 | tf_op jit(solution)/shard_map/pallas_call | solution.py:125
  98.5 2.9 %collective-permute-start.7 = (bf16[512,256]{1,0:T(8,128)(2,1)S(1)}, bf16[512,256]{1,0:T(8,128)(2,1)S(1)}, u32[]{:S(2)}, u32[]{:S(2)}) collective-permute-start(bf16[512,256]{1,0:T(8,128)(2,1)S(1)} %get-tuple-element.25), channel_id=1, source_target_pairs={{0,7},{1,6},{2,5},{3,4},{4,3},{5,2},{6,1},{7,0},{8,15},{9,14},{10,... | collective-permute-start | bytes 786440 | tf_op jit(solution)/shard_map/ppermute | solution.py:192
  101.5 8.2 %shard_map.65 = (bf16[512,256]{1,0:T(8,128)(2,1)S(1)}, bf16[512,256]{1,0:T(8,128)(2,1)S(1)}) custom-call(f32[2,256,1280]{2,1,0:T(8,128)S(1)} %fusion.4.bias_ref, bf16[256,256]{1,0:T(8,128)(2,1)S(1)} %rev.4.flip_ref, bf16[512,3072]{1,0:T(8,128)(2,1)} %copy-done, bf16[1024,2048]{1,0:T(8,128)(2,1)} %shard_map.60.kl.kr.vl.vr, bf16[512,3072]{1,0:T(8,128)(2,1)} %copy-done, ...), custom_call_target="tpu_custom_call" | custom-call | flops 2684354560 | bytes 5242880 | tf_op jit(solution)/shard_map/pallas_call | solution.py:125
  109.7 0.1 collective-permute-start.8
  109.8 8.2 %shard_map.61 = (bf16[512,256]{1,0:T(8,128)(2,1)S(1)}, bf16[512,256]{1,0:T(8,128)(2,1)S(1)}) custom-call(f32[2,256,1280]{2,1,0:T(8,128)S(1)} %fusion.4.bias_ref, bf16[256,256]{1,0:T(8,128)(2,1)S(1)} %rev.4.flip_ref, bf16[512,3072]{1,0:T(8,128)(2,1)} %copy-done, bf16[1024,2048]{1,0:T(8,128)(2,1)} %shard_map.60.kl.kr.vl.vr, bf16[512,3072]{1,0:T(8,128)(2,1)} %copy-done, ...), custom_call_target="tpu_custom_call" | custom-call | flops 2684354560 | bytes 5242880 | tf_op jit(solution)/shard_map/pallas_call | solution.py:125
  118.1 1.8 collective-permute-start.6
  119.8 0.1 collective-permute-start.5
  119.9 1.7 collective-permute-start.4
  121.6 0.1 collective-permute-start.9
  121.7 0.1 add_convert_fusion.4
  121.7 36.5 %collective-permute-done.8 = bf16[512,256]{1,0:T(8,128)(2,1)S(1)} collective-permute-done((bf16[512,256]{1,0:T(8,128)(2,1)S(1)}, bf16[512,256]{1,0:T(8,128)(2,1)S(1)}, u32[]{:S(2)}, u32[]{:S(2)}) %collective-permute-start.8) | collective-permute-done | bytes 262176 | tf_op jit(solution)/shard_map/ppermute | solution.py:192
  158.2 1.9 collective-permute-start.10
  160.2 0.1 add_convert_fusion.3
  160.2 3.6 %collective-permute-done.6 = bf16[512,256]{1,0:T(8,128)(2,1)S(1)} collective-permute-done((bf16[512,256]{1,0:T(8,128)(2,1)S(1)}, bf16[512,256]{1,0:T(8,128)(2,1)S(1)}, u32[]{:S(2)}, u32[]{:S(2)}) %collective-permute-start.6) | collective-permute-done | bytes 262176 | tf_op jit(solution)/shard_map/ppermute | solution.py:192
  163.9 1.9 collective-permute-start.11
  165.8 0.1 add_convert_fusion.5
  165.9 14.9 %collective-permute-done.9 = bf16[512,256]{1,0:T(8,128)(2,1)S(1)} collective-permute-done((bf16[512,256]{1,0:T(8,128)(2,1)S(1)}, bf16[512,256]{1,0:T(8,128)(2,1)S(1)}, u32[]{:S(2)}, u32[]{:S(2)}) %collective-permute-start.9) | collective-permute-done | bytes 262176 | tf_op jit(solution)/shard_map/ppermute | solution.py:192
  180.7 0.1 add_convert_fusion.2
  180.8 0.1 add_convert_fusion.7
  180.9 0.1 add_convert_fusion.6
  181.0 1.1 pad_maximum_fusion
  182.1 4.3 %collective-permute-done.10 = bf16[512,256]{1,0:T(8,128)(2,1)S(1)} collective-permute-done((bf16[512,256]{1,0:T(8,128)(2,1)S(1)}, bf16[512,256]{1,0:T(8,128)(2,1)S(1)}, u32[]{:S(2)}, u32[]{:S(2)}) %collective-permute-start.10) | collective-permute-done | bytes 262176 | tf_op jit(solution)/shard_map/ppermute | solution.py:192
  186.3 0.1 add_convert_fusion.1
  186.4 5.5 %collective-permute-done.11 = bf16[512,256]{1,0:T(8,128)(2,1)S(1)} collective-permute-done((bf16[512,256]{1,0:T(8,128)(2,1)S(1)}, bf16[512,256]{1,0:T(8,128)(2,1)S(1)}, u32[]{:S(2)}, u32[]{:S(2)}) %collective-permute-start.11) | collective-permute-done | bytes 262176 | tf_op jit(solution)/shard_map/ppermute | solution.py:192
  191.9 0.1 add_convert_fusion
  192.0 1.1 pad_maximum_fusion.1
  (12 shorter events, 0.0 us)
Async XLA Ops:
  0.6 72.6 %collective-permute-start.1 = (bf16[512,1024]{1,0:T(8,128)(2,1)}, bf16[512,1024]{1,0:T(8,128)(2,1)S(1)}, u32[]{:S(2)}, u32[]{:S(2)}) collective-permute-start(bf16[512,1024]{1,0:T(8,128)(2,1)} %refs_0_.2), channel_id=1, source_target_pairs={{1,0},{2,1},{3,2},{4,3},{5,4},{6,5},{7,6},{9,8},{10,9},{11,10},{12... | collective-permute-start | bytes 3145736 | tf_op jit(solution)/shard_map/ppermute | solution.py:181
  2.6 70.7 %collective-permute-start = (bf16[512,1024]{1,0:T(8,128)(2,1)}, bf16[512,1024]{1,0:T(8,128)(2,1)S(1)}, u32[]{:S(2)}, u32[]{:S(2)}) collective-permute-start(bf16[512,1024]{1,0:T(8,128)(2,1)} %refs_0_.2), channel_id=1, source_target_pairs={{0,1},{1,2},{2,3},{3,4},{4,5},{5,6},{6,7},{8,9},{9,10},{10,11},{11... | collective-permute-start | bytes 3145736 | tf_op jit(solution)/shard_map/ppermute | solution.py:180
  5.0 25.8 %collective-permute-start.3 = (bf16[512,1024]{1,0:T(8,128)(2,1)}, bf16[512,1024]{1,0:T(8,128)(2,1)}, u32[]{:S(2)}, u32[]{:S(2)}) collective-permute-start(bf16[512,1024]{1,0:T(8,128)(2,1)} %refs_0_.3), channel_id=1, source_target_pairs={{1,0},{2,1},{3,2},{4,3},{5,4},{6,5},{7,6},{9,8},{10,9},{11,10},{12... | collective-permute-start | bytes 3145736 | tf_op jit(solution)/shard_map/ppermute | solution.py:181
  8.1 22.6 %collective-permute-start.2 = (bf16[512,1024]{1,0:T(8,128)(2,1)}, bf16[512,1024]{1,0:T(8,128)(2,1)}, u32[]{:S(2)}, u32[]{:S(2)}) collective-permute-start(bf16[512,1024]{1,0:T(8,128)(2,1)} %refs_0_.3), channel_id=1, source_target_pairs={{0,1},{1,2},{2,3},{3,4},{4,5},{5,6},{6,7},{8,9},{9,10},{10,11},{11... | collective-permute-start | bytes 3145736 | tf_op jit(solution)/shard_map/ppermute | solution.py:180
  11.0 1.2 copy-start.2
  12.2 9.1 %copy-start.3 = (bf16[512,1024]{1,0:T(8,128)(2,1)S(1)}, bf16[512,1024]{1,0:T(8,128)(2,1)}, u32[]{:S(2)}) copy-start(bf16[512,1024]{1,0:T(8,128)(2,1)} %refs_0_.2) | copy-start | bytes 3145732
  19.5 1.8 copy-start.1
  28.5 1.7 copy-start
  98.5 23.1 %collective-permute-start.7 = (bf16[512,256]{1,0:T(8,128)(2,1)S(1)}, bf16[512,256]{1,0:T(8,128)(2,1)S(1)}, u32[]{:S(2)}, u32[]{:S(2)}) collective-permute-start(bf16[512,256]{1,0:T(8,128)(2,1)S(1)} %get-tuple-element.25), channel_id=1, source_target_pairs={{0,7},{1,6},{2,5},{3,4},{4,3},{5,2},{6,1},{7,0},{8,15},{9,14},{10,... | collective-permute-start | bytes 786440 | tf_op jit(solution)/shard_map/ppermute | solution.py:192
  109.7 48.5 %collective-permute-start.8 = (bf16[512,256]{1,0:T(8,128)(2,1)S(1)}, bf16[512,256]{1,0:T(8,128)(2,1)S(1)}, u32[]{:S(2)}, u32[]{:S(2)}) collective-permute-start(bf16[512,256]{1,0:T(8,128)(2,1)S(1)} %get-tuple-element.27), channel_id=1, source_target_pairs={{0,7},{1,6},{2,5},{3,4},{4,3},{5,2},{6,1},{7,0},{8,15},{9,14},{10,... | collective-permute-start | bytes 786440 | tf_op jit(solution)/shard_map/ppermute | solution.py:192
  118.1 45.8 %collective-permute-start.6 = (bf16[512,256]{1,0:T(8,128)(2,1)S(1)}, bf16[512,256]{1,0:T(8,128)(2,1)S(1)}, u32[]{:S(2)}, u32[]{:S(2)}) collective-permute-start(bf16[512,256]{1,0:T(8,128)(2,1)S(1)} %get-tuple-element.23), channel_id=1, source_target_pairs={{0,7},{1,6},{2,5},{3,4},{4,3},{5,2},{6,1},{7,0},{8,15},{9,14},{10,... | collective-permute-start | bytes 786440 | tf_op jit(solution)/shard_map/ppermute | solution.py:192
  119.8 61.0 %collective-permute-start.5 = (bf16[512,256]{1,0:T(8,128)(2,1)S(1)}, bf16[512,256]{1,0:T(8,128)(2,1)S(1)}, u32[]{:S(2)}, u32[]{:S(2)}) collective-permute-start(bf16[512,256]{1,0:T(8,128)(2,1)S(1)} %get-tuple-element.21), channel_id=1, source_target_pairs={{0,7},{1,6},{2,5},{3,4},{4,3},{5,2},{6,1},{7,0},{8,15},{9,14},{10,... | collective-permute-start | bytes 786440 | tf_op jit(solution)/shard_map/ppermute | solution.py:192
  119.9 60.9 %collective-permute-start.4 = (bf16[512,256]{1,0:T(8,128)(2,1)S(1)}, bf16[512,256]{1,0:T(8,128)(2,1)S(1)}, u32[]{:S(2)}, u32[]{:S(2)}) collective-permute-start(bf16[512,256]{1,0:T(8,128)(2,1)S(1)} %get-tuple-element.19), channel_id=1, source_target_pairs={{0,7},{1,6},{2,5},{3,4},{4,3},{5,2},{6,1},{7,0},{8,15},{9,14},{10,... | collective-permute-start | bytes 786440 | tf_op jit(solution)/shard_map/ppermute | solution.py:192
  121.6 59.1 %collective-permute-start.9 = (bf16[512,256]{1,0:T(8,128)(2,1)S(1)}, bf16[512,256]{1,0:T(8,128)(2,1)S(1)}, u32[]{:S(2)}, u32[]{:S(2)}) collective-permute-start(bf16[512,256]{1,0:T(8,128)(2,1)S(1)} %get-tuple-element.29), channel_id=1, source_target_pairs={{0,7},{1,6},{2,5},{3,4},{4,3},{5,2},{6,1},{7,0},{8,15},{9,14},{10,... | collective-permute-start | bytes 786440 | tf_op jit(solution)/shard_map/ppermute | solution.py:192
  158.2 28.1 %collective-permute-start.10 = (bf16[512,256]{1,0:T(8,128)(2,1)S(1)}, bf16[512,256]{1,0:T(8,128)(2,1)S(1)}, u32[]{:S(2)}, u32[]{:S(2)}) collective-permute-start(bf16[512,256]{1,0:T(8,128)(2,1)S(1)} %get-tuple-element.31), channel_id=1, source_target_pairs={{0,7},{1,6},{2,5},{3,4},{4,3},{5,2},{6,1},{7,0},{8,15},{9,14},{10,... | collective-permute-start | bytes 786440 | tf_op jit(solution)/shard_map/ppermute | solution.py:192
  163.9 28.1 %collective-permute-start.11 = (bf16[512,256]{1,0:T(8,128)(2,1)S(1)}, bf16[512,256]{1,0:T(8,128)(2,1)S(1)}, u32[]{:S(2)}, u32[]{:S(2)}) collective-permute-start(bf16[512,256]{1,0:T(8,128)(2,1)S(1)} %get-tuple-element.33), channel_id=1, source_target_pairs={{0,7},{1,6},{2,5},{3,4},{4,3},{5,2},{6,1},{7,0},{8,15},{9,14},{10,... | collective-permute-start | bytes 786440 | tf_op jit(solution)/shard_map/ppermute | solution.py:192

commit v2 on v0

v2 whole, which is shorter than its diff:
```python
import functools
import math

import jax
import jax.numpy as jnp
from jax import lax
from jax.experimental import pallas as pl
from jax.experimental.pallas import tpu as pltpu
from jax.sharding import PartitionSpec as P

HEADS = 16
WINDOW = 512
BLOCK = 256
TILE = 256
LANES = 128
FAR = -1e30
MESH = pl.DeviceIdType.MESH


def kernel(
    count, scale, gain_ref, xf_ref, xr_ref, w_ref, y_ref,
    x_own, x_halo, w_vmem, hn, qkv, kx, vx, bias, band, flip, turned, arrived,
    load_sem, halo_send, halo_recv, turn_send, turn_recv,
):
    rows = xf_ref.shape[0]
    width = xf_ref.shape[1]
    pairs = width // LANES
    blocks = rows // BLOCK
    ext = rows + 2 * WINDOW
    span = 2 * WINDOW + BLOCK
    me = lax.axis_index("seq")
    left, right, across = me - 1, me + 1, count - 1 - me
    has_left, has_right = me > 0, me < count - 1
    x_refs = (xf_ref, xr_ref)

    loads = [
        pltpu.make_async_copy(xf_ref, x_own.at[0], load_sem.at[0]),
        pltpu.make_async_copy(w_ref, w_vmem, load_sem.at[2]),
        pltpu.make_async_copy(xr_ref, x_own.at[1], load_sem.at[1]),
    ]
    for copy in loads:
        copy.start()

    barrier = pltpu.get_barrier_semaphore()

    @pl.when(has_left)
    def _():
        pl.semaphore_signal(barrier, inc=1, device_id={"seq": left}, device_id_type=MESH)

    @pl.when(has_right)
    def _():
        pl.semaphore_signal(barrier, inc=1, device_id={"seq": right}, device_id_type=MESH)

    pl.semaphore_signal(barrier, inc=1, device_id={"seq": across}, device_id_type=MESH)
    pl.semaphore_wait(barrier, 1 + jnp.where(has_left, 1, 0) + jnp.where(has_right, 1, 0))

    def to_right(strand):
        return pltpu.make_async_remote_copy(
            src_ref=x_refs[strand].at[pl.ds(rows - WINDOW, WINDOW)],
            dst_ref=x_halo.at[strand, pl.ds(0, WINDOW)],
            send_sem=halo_send.at[strand, 0],
            recv_sem=halo_recv.at[strand, 0],
            device_id={"seq": right},
            device_id_type=MESH,
        )

    def to_left(strand):
        return pltpu.make_async_remote_copy(
            src_ref=x_refs[strand].at[pl.ds(0, WINDOW)],
            dst_ref=x_halo.at[strand, pl.ds(WINDOW, WINDOW)],
            send_sem=halo_send.at[strand, 1],
            recv_sem=halo_recv.at[strand, 1],
            device_id={"seq": left},
            device_id_type=MESH,
        )

    def send_halo(strand):
        @pl.when(has_right)
        def _():
            to_right(strand).start()

        @pl.when(has_left)
        def _():
            to_left(strand).start()

    def across_copy(strand, pair):
        return pltpu.make_async_remote_copy(
            src_ref=turned.at[strand, pair],
            dst_ref=arrived.at[strand, pair],
            send_sem=turn_send.at[strand, pair],
            recv_sem=turn_recv.at[strand, pair],
            device_id={"seq": across},
            device_id_type=MESH,
        )

    send_halo(0)

    @pl.when(jnp.logical_not(has_left))
    def _():
        x_halo[:, :WINDOW, :] = jnp.zeros((2, WINDOW, width), jnp.bfloat16)

    @pl.when(jnp.logical_not(has_right))
    def _():
        x_halo[:, WINDOW:, :] = jnp.zeros((2, WINDOW, width), jnp.bfloat16)

    row = lax.broadcasted_iota(jnp.int32, (BLOCK, BLOCK), 0)
    col = lax.broadcasted_iota(jnp.int32, (BLOCK, BLOCK), 1)
    band[0] = jnp.where(col >= row, 0.0, FAR)
    band[1] = jnp.where(col <= row, 0.0, FAR)
    flip[...] = jnp.where(col + row == BLOCK - 1, 1.0, 0.0).astype(jnp.bfloat16)
    key = lax.broadcasted_iota(jnp.int32, (ext, LANES), 0)
    first = jnp.where(has_left, 0, WINDOW)
    last = jnp.where(has_right, ext, WINDOW + rows)
    bias[...] = jnp.where((key >= first) & (key < last), 0.0, FAR).astype(jnp.bfloat16)

    def normalise(source, strand, total):
        def step(i, carry):
            at = pl.ds(pl.multiple_of(i * LANES, LANES), LANES)
            xf = source[strand, at, :].astype(jnp.float32)
            meansq = jnp.mean(xf * xf, axis=-1, keepdims=True)
            out = xf * lax.rsqrt(meansq + 1e-06) * gain_ref[...].astype(jnp.float32)
            hn[at, :] = out.astype(jnp.bfloat16)
            return carry

        lax.fori_loop(0, total // LANES, step, 0)

    def project_own(strand, carry):
        normalise(x_own, strand, rows)

        def step(j, carry):
            at = pl.ds(pl.multiple_of(j * TILE, TILE), TILE)
            out = jnp.dot(hn[:rows, :], w_vmem[:, at], preferred_element_type=jnp.float32)
            out = out * jnp.where(j < width // TILE, scale, 1.0)
            qkv[strand, WINDOW:WINDOW + rows, at] = out.astype(jnp.bfloat16)
            return carry

        return lax.fori_loop(0, 3 * width // TILE, step, carry)

    def project_halo(strand):
        normalise(x_halo, strand, 2 * WINDOW)

        def step(j, carry):
            at = pl.ds(pl.multiple_of(j * TILE, TILE), TILE)
            out = jnp.dot(hn[:2 * WINDOW, :], w_vmem[:, at], preferred_element_type=jnp.float32)
            out = out.astype(jnp.bfloat16)
            qkv[strand, :WINDOW, at] = out[:WINDOW]
            qkv[strand, WINDOW + rows:, at] = out[WINDOW:]
            return carry

        lax.fori_loop(width // TILE, 3 * width // TILE, step, 0)

    low = lax.broadcasted_iota(jnp.int32, (BLOCK, LANES), 1) < LANES // 2
    lane = lax.broadcasted_iota(jnp.int32, (BLOCK, LANES), 1)

    def attend(strand, pair):
        columns = [
            pl.ds(pl.multiple_of(pair * LANES + part * width, LANES), LANES) for part in range(3)
        ]

        def lay(i, carry):
            at = pl.ds(pl.multiple_of(i * BLOCK, BLOCK), BLOCK)
            k = qkv[strand, at, columns[1]]
            v = qkv[strand, at, columns[2]]
            side = bias[at, :]
            one = jnp.ones_like(v)
            kx[0, at, :] = jnp.where(low, k, side)
            kx[1, at, :] = jnp.where(low, side, k)
            vx[0, at, :] = jnp.where(low, v, one)
            vx[1, at, :] = jnp.where(low, one, v)
            return carry

        lax.fori_loop(0, ext // BLOCK, lay, 0)

        def block_step(block, carry):
            start = pl.multiple_of(block * BLOCK, BLOCK)
            q = qkv[strand, pl.ds(pl.multiple_of(WINDOW + start, BLOCK), BLOCK), columns[0]]
            outs = []
            for head in range(2):
                mark = jnp.where(lane == (LANES // 2 if head == 0 else 0), 1.0, 0.0).astype(jnp.bfloat16)
                qh = jnp.where(low if head == 0 else jnp.logical_not(low), q, mark)
                cuts = ((0, BLOCK), (BLOCK, 2 * WINDOW - BLOCK), (2 * WINDOW, BLOCK))
                scores = []
                for offset, size in cuts:
                    at = pl.ds(pl.multiple_of(start + offset, BLOCK), size)
                    scores.append(
                        lax.dot_general(
                            qh, kx[head, at, :], (((1,), (1,)), ((), ())),
                            preferred_element_type=jnp.float32,
                        )
                    )
                scores[0] = scores[0] + band[0]
                scores[2] = scores[2] + band[1]
                top = jnp.max(scores[1], axis=-1, keepdims=True)
                top = jnp.maximum(top, jnp.max(jnp.maximum(scores[0], scores[2]), axis=-1, keepdims=True))
                p = jnp.concatenate(
                    [jnp.exp2(s - top).astype(jnp.bfloat16) for s in scores], axis=1
                )
                outs.append(
                    jnp.dot(p, vx[head, pl.ds(start, span), :], preferred_element_type=jnp.float32)
                )
            num = jnp.where(low, outs[0], outs[1])
            den = pltpu.roll(jnp.where(low, outs[1], outs[0]), LANES // 2, 1)
            a = (num / den).astype(jnp.bfloat16)
            y_ref[strand, pl.ds(start, BLOCK), columns[0]] = a
            back = jnp.dot(flip[...], a, preferred_element_type=jnp.float32).astype(jnp.bfloat16)
            back = jnp.dot(
                back, flip[:LANES, BLOCK - LANES:], preferred_element_type=jnp.float32
            ).astype(jnp.bfloat16)
            other = pl.ds(pl.multiple_of((blocks - 1 - block) * BLOCK, BLOCK), BLOCK)
            turned[strand, pair, other, :] = back
            return carry

        lax.fori_loop(0, blocks, block_step, 0)
        across_copy(strand, pair).start()

    loads[0].wait()
    loads[1].wait()
    project_own(0, 0)
    send_halo(1)
    loads[2].wait()
    project_own(1, 0)

    def strand_step(strand):
        @pl.when(has_left)
        def _():
            to_right(strand).wait_recv()

        @pl.when(has_right)
        def _():
            to_left(strand).wait_recv()

        project_halo(strand)

        def pair_step(pair, carry):
            attend(strand, pair)
            return carry

        lax.fori_loop(0, pairs, pair_step, 0)

    strand_step(0)
    strand_step(1)

    def combine(strand):
        def step(pair, carry):
            across_copy(1 - strand, pair).wait_recv()
            columns = pl.ds(pl.multiple_of((pairs - 1 - pair) * LANES, LANES), LANES)
            near = y_ref[strand, :, columns].astype(jnp.float32)
            far = arrived[1 - strand, pair].astype(jnp.float32)
            y_ref[strand, :, columns] = (near + far).astype(jnp.bfloat16)
            return carry

        lax.fori_loop(0, pairs, step, 0)

    combine(1)
    combine(0)

    def finish(pair, carry):
        across_copy(0, pair).wait_send()
        across_copy(1, pair).wait_send()
        return carry

    lax.fori_loop(0, pairs, finish, 0)
    for strand in range(2):
        @pl.when(has_right)
        def _():
            to_right(strand).wait_send()

        @pl.when(has_left)
        def _():
            to_left(strand).wait_send()


def per_device(x_fwd, x_rev, gain, w_qkv):
    rows, width = x_fwd.shape
    count = lax.axis_size("seq")
    pairs = width // LANES
    ext = rows + 2 * WINDOW
    scale = (width // HEADS) ** (-0.5) * math.log2(math.e)
    anywhere = pl.BlockSpec(memory_space=pl.ANY)
    inside = pl.BlockSpec(memory_space=pltpu.VMEM)
    half = jnp.bfloat16
    y = pl.pallas_call(
        functools.partial(kernel, count, scale),
        in_specs=[inside, anywhere, anywhere, anywhere],
        out_specs=inside,
        out_shape=jax.ShapeDtypeStruct((2, rows, width), half),
        scratch_shapes=[
            pltpu.VMEM((2, rows, width), half),
            pltpu.VMEM((2, 2 * WINDOW, width), half),
            pltpu.VMEM((width, 3 * width), half),
            pltpu.VMEM((max(rows, 2 * WINDOW), width), half),
            pltpu.VMEM((2, ext, 3 * width), half),
            pltpu.VMEM((2, ext, LANES), half),
            pltpu.VMEM((2, ext, LANES), half),
            pltpu.VMEM((ext, LANES), half),
            pltpu.VMEM((2, BLOCK, BLOCK), jnp.float32),
            pltpu.VMEM((BLOCK, BLOCK), half),
            pltpu.VMEM((2, pairs, rows, LANES), half),
            pltpu.VMEM((2, pairs, rows, LANES), half),
            pltpu.SemaphoreType.DMA((3,)),
            pltpu.SemaphoreType.DMA((2, 2)),
            pltpu.SemaphoreType.DMA((2, 2)),
            pltpu.SemaphoreType.DMA((2, pairs)),
            pltpu.SemaphoreType.DMA((2, pairs)),
        ],
        compiler_params=pltpu.CompilerParams(
            collective_id=0, has_side_effects=True, vmem_limit_bytes=62 * 1024 * 1024
        ),
        cost_estimate=pl.CostEstimate(
            flops=2 * rows * width * 3 * width * 4,
            bytes_accessed=2 * (4 * rows * width + 3 * width * width),
            transcendentals=2 * HEADS * rows * (2 * WINDOW + BLOCK),
        ),
    )(gain.reshape(1, -1), x_fwd, x_rev, w_qkv)
    return y[0], y[1]


def solution(mesh):
    in_specs = (P(("dp", "seq"), None), P(("dp", "seq"), None), P(), P())
    out_specs = (P(("dp", "seq"), None), P(("dp", "seq"), None))
    return jax.shard_map(
        per_device, mesh=mesh, in_specs=in_specs, out_specs=out_specs, check_vma=False
    )
```

time: 369 us -> 126 us (0.34)
  the two profiles are of different devices: /device:TPU:0 before, /device:TPU:12 now
where the time goes in v2:
time: 126 us; the launch traced here: 125 us
  Pallas kernels  120 us (95%)
  local copies, waits for them, and re-layouts  4.31 us (3%)
    pallas_call x1, Pallas kernels, per_device(): pl.pallas_call(functools.partial(kernel, count, scale), in_specs=[inside,...  120 us
    squeeze x1, local copies, waits for them, and re-layouts, per_device(): return (y[0], y[1])  3.03 us

profile of v2, /device:TPU:12, one launch (start us, length us, event | category | flops | bytes accessed | tf_op | source)
XLA Modules:
  0.0 124.6 jit_solution(7294833287846772229)
XLA Ops:
  0.6 1.3 %reshape.7.gain_ref = bf16[1,1024]{1,0:T(2,128)(2,1)} reshape(bf16[1024]{0:T(1024)(128)(2,1)} %param.6) | data formatting | bytes 4096 | tf_op jit(solution)/shard_map/reshape | solution.py:314
  1.9 119.7 %shard_map.59 = bf16[2,512,1024]{2,1,0:T(8,128)(2,1)} custom-call(bf16[1,1024]{1,0:T(2,128)(2,1)} %reshape.7.gain_ref, bf16[512,1024]{1,0:T(8,128)(2,1)} %xf_ref.1, bf16[512,1024]{1,0:T(8,128)(2,1)} %xr_ref.1, bf16[1024,3072]{1,0:T(8,128)(2,1)} %w_ref.1), custom_call_target="tpu_custom_call" | custom-call | flops 12884901888 | bytes 10485760 | tf_op jit(solution)/shard_map/pallas_call | solution.py:282
  121.6 3.0 %slice_bitcast_fusion = (bf16[512,1024]{1,0:T(8,128)(2,1)}, bf16[512,1024]{1,0:T(8,128)(2,1)}) fusion(bf16[2,512,1024]{2,1,0:T(8,128)(2,1)} %shard_map.59), kind=kLoop, calls=%fused_computation | loop fusion | bytes 4194304 | tf_op jit(solution)/shard_map/squeeze | solution.py:315

commit v3 on v2

v3 whole, which is shorter than its diff:
```python
import functools
import math

import jax
import jax.numpy as jnp
from jax import lax
from jax.experimental import pallas as pl
from jax.experimental.pallas import tpu as pltpu
from jax.sharding import PartitionSpec as P

HEADS = 16
WINDOW = 512
BLOCK = 256
TILE = 256
LANES = 128
FAR = -1e30
MESH = pl.DeviceIdType.MESH


def kernel(
    count, scale, gain_ref, xf_ref, xr_ref, w_ref, yf_ref, yr_ref,
    x_own, x_halo, w_vmem, hn, qkv, kx, vx, bias, band, flip, turned,
    load_sem, halo_send, halo_recv, cross_send, cross_recv, pass_send, pass_recv, back_send, back_recv,
):
    rows = xf_ref.shape[0]
    width = xf_ref.shape[1]
    pairs = width // LANES
    blocks = rows // BLOCK
    chunks = rows // LANES
    ext = rows + 2 * WINDOW
    span = 2 * WINDOW + BLOCK
    me = lax.axis_index("seq")
    left, right, across = me - 1, me + 1, count - 1 - me
    has_left, has_right = me > 0, me < count - 1
    no_left, no_right = me == 0, me == count - 1
    mid_low, mid_high = me == count // 2 - 1, me == count // 2
    pass_left = has_left & (me != count // 2)
    pass_right = has_right & (me != count // 2 - 1)

    load_x = pltpu.make_async_copy(xf_ref, x_own.at[0], load_sem.at[0])
    load_w = pltpu.make_async_copy(w_ref, w_vmem, load_sem.at[1])
    keep_low = pltpu.make_async_copy(
        xr_ref.at[pl.ds(rows - WINDOW, WINDOW)], x_halo.at[1, pl.ds(0, WINDOW)], load_sem.at[2]
    )
    keep_high = pltpu.make_async_copy(
        xr_ref.at[pl.ds(0, WINDOW)], x_halo.at[1, pl.ds(WINDOW, WINDOW)], load_sem.at[2]
    )
    load_x.start()
    load_w.start()

    barrier = pltpu.get_barrier_semaphore()

    @pl.when(has_left)
    def _():
        pl.semaphore_signal(barrier, inc=1, device_id={"seq": left}, device_id_type=MESH)

    @pl.when(has_right)
    def _():
        pl.semaphore_signal(barrier, inc=1, device_id={"seq": right}, device_id_type=MESH)

    pl.semaphore_signal(barrier, inc=1, device_id={"seq": across}, device_id_type=MESH)
    pl.semaphore_wait(barrier, 1 + jnp.where(has_left, 1, 0) + jnp.where(has_right, 1, 0))

    def remote(src, dst, send, recv, device):
        return pltpu.make_async_remote_copy(
            src_ref=src, dst_ref=dst, send_sem=send, recv_sem=recv,
            device_id={"seq": device}, device_id_type=MESH,
        )

    def to_right():
        return remote(
            xf_ref.at[pl.ds(rows - WINDOW, WINDOW)], x_halo.at[0, pl.ds(0, WINDOW)],
            halo_send.at[0], halo_recv.at[0], right,
        )

    def to_left():
        return remote(
            xf_ref.at[pl.ds(0, WINDOW)], x_halo.at[0, pl.ds(WINDOW, WINDOW)],
            halo_send.at[1], halo_recv.at[1], left,
        )

    def cross(chunk):
        at = pl.ds(chunk * LANES, LANES)
        return remote(xr_ref.at[at], x_own.at[1, at], cross_send.at[chunk], cross_recv.at[chunk], across)

    near_left = [c for c in range(chunks) if c * LANES >= rows - WINDOW]
    near_right = [c for c in range(chunks) if c * LANES < WINDOW]

    def hand_left(chunk):
        at = pl.ds(chunk * LANES, LANES)
        to = pl.ds(chunk * LANES - (rows - WINDOW), LANES)
        return remote(
            x_own.at[1, at], x_halo.at[1, to], pass_send.at[0, chunk], pass_recv.at[0, chunk], left
        )

    def hand_right(chunk):
        at = pl.ds(chunk * LANES, LANES)
        to = pl.ds(WINDOW + chunk * LANES, LANES)
        return remote(
            x_own.at[1, at], x_halo.at[1, to], pass_send.at[1, chunk], pass_recv.at[1, chunk], right
        )

    def columns_of(pair):
        return pl.ds(pl.multiple_of(pair * LANES, LANES), LANES)

    def send_back(pair):
        return remote(
            turned.at[pair], yr_ref.at[:, columns_of(pair)],
            back_send.at[pair], back_recv.at[pair], across,
        )

    pl.when(has_right)(lambda: to_right().start())
    pl.when(has_left)(lambda: to_left().start())
    pl.when(mid_low)(lambda: keep_low.start())
    pl.when(mid_high)(lambda: keep_high.start())

    @pl.when(no_left)
    def _():
        x_halo[0, :WINDOW, :] = jnp.zeros((WINDOW, width), jnp.bfloat16)
        x_halo[1, WINDOW:, :] = jnp.zeros((WINDOW, width), jnp.bfloat16)

    @pl.when(no_right)
    def _():
        x_halo[0, WINDOW:, :] = jnp.zeros((WINDOW, width), jnp.bfloat16)
        x_halo[1, :WINDOW, :] = jnp.zeros((WINDOW, width), jnp.bfloat16)

    row = lax.broadcasted_iota(jnp.int32, (BLOCK, BLOCK), 0)
    col = lax.broadcasted_iota(jnp.int32, (BLOCK, BLOCK), 1)
    band[0] = jnp.where(col >= row, 0.0, FAR)
    band[1] = jnp.where(col <= row, 0.0, FAR)
    flip[...] = jnp.where(col + row == BLOCK - 1, 1.0, 0.0).astype(jnp.bfloat16)
    key = lax.broadcasted_iota(jnp.int32, (ext, LANES), 0)
    for strand, (before, after) in enumerate(((has_left, has_right), (has_right, has_left))):
        first = jnp.where(before, 0, WINDOW)
        last = jnp.where(after, ext, WINDOW + rows)
        bias[strand] = jnp.where((key >= first) & (key < last), 0.0, FAR).astype(jnp.bfloat16)

    def project(source, strand, src, dst, total, first_tile):
        def normalise(i, carry):
            at = pl.ds(pl.multiple_of(src + i * LANES, LANES), LANES)
            xf = source[strand, at, :].astype(jnp.float32)
            meansq = jnp.mean(xf * xf, axis=-1, keepdims=True)
            out = xf * lax.rsqrt(meansq + 1e-06) * gain_ref[...].astype(jnp.float32)
            hn[pl.ds(pl.multiple_of(i * LANES, LANES), LANES), :] = out.astype(jnp.bfloat16)
            return carry

        lax.fori_loop(0, total // LANES, normalise, 0)

        def step(j, carry):
            at = pl.ds(pl.multiple_of(j * TILE, TILE), TILE)
            out = jnp.dot(hn[:total, :], w_vmem[:, at], preferred_element_type=jnp.float32)
            out = out * jnp.where(j < width // TILE, scale, 1.0)
            qkv[strand, pl.ds(pl.multiple_of(dst, LANES), total), at] = out.astype(jnp.bfloat16)
            return carry

        lax.fori_loop(first_tile, 3 * width // TILE, step, 0)

    def project_side(strand, side):
        project(x_halo, strand, side * WINDOW, side * (WINDOW + rows), WINDOW, width // TILE)

    lane = lax.broadcasted_iota(jnp.int32, (BLOCK, LANES), 1)
    low = lane < LANES // 2

    def attend(strand, pair):
        columns = [columns_of(pair + part * pairs) for part in range(3)]

        def lay(i, carry):
            at = pl.ds(pl.multiple_of(i * BLOCK, BLOCK), BLOCK)
            k = qkv[strand, at, columns[1]]
            v = qkv[strand, at, columns[2]]
            side = bias[strand, at, :]
            one = jnp.ones_like(v)
            kx[0, at, :] = jnp.where(low, k, side)
            kx[1, at, :] = jnp.where(low, side, k)
            vx[0, at, :] = jnp.where(low, v, one)
            vx[1, at, :] = jnp.where(low, one, v)
            return carry

        lax.fori_loop(0, ext // BLOCK, lay, 0)

        def block_step(block, carry):
            start = pl.multiple_of(block * BLOCK, BLOCK)
            here = pl.ds(start, BLOCK)
            q = qkv[strand, pl.ds(pl.multiple_of(WINDOW + start, BLOCK), BLOCK), columns[0]]
            cuts = ((0, BLOCK), (BLOCK, 2 * WINDOW - BLOCK), (2 * WINDOW, BLOCK))
            scores = []
            for head in range(2):
                mark = jnp.where(lane == (LANES // 2 if head == 0 else 0), 1.0, 0.0).astype(jnp.bfloat16)
                qh = jnp.where(low if head == 0 else jnp.logical_not(low), q, mark)
                scores.append(
                    [
                        lax.dot_general(
                            qh, kx[head, pl.ds(pl.multiple_of(start + offset, BLOCK), size), :],
                            (((1,), (1,)), ((), ())), preferred_element_type=jnp.float32,
                        )
                        for offset, size in cuts
                    ]
                )
            outs = []
            for head in range(2):
                one, two, three = scores[head]
                one = one + band[0]
                three = three + band[1]
                top = jnp.max(two, axis=-1, keepdims=True)
                top = jnp.maximum(top, jnp.max(jnp.maximum(one, three), axis=-1, keepdims=True))
                p = jnp.concatenate(
                    [jnp.exp2(s - top).astype(jnp.bfloat16) for s in (one, two, three)], axis=1
                )
                outs.append(
                    jnp.dot(p, vx[head, pl.ds(start, span), :], preferred_element_type=jnp.float32)
                )
            num = jnp.where(low, outs[0], outs[1])
            den = pltpu.roll(jnp.where(low, outs[1], outs[0]), LANES // 2, 1)
            a = (num / den).astype(jnp.bfloat16)
            back = jnp.dot(flip[...], a, preferred_element_type=jnp.float32).astype(jnp.bfloat16)
            back = jnp.dot(back, flip[:LANES, BLOCK - LANES:], preferred_element_type=jnp.float32)
            other = pl.ds(pl.multiple_of((blocks - 1 - block) * BLOCK, BLOCK), BLOCK)
            if strand == 0:
                yf_ref[here, columns[0]] = a
                turned[pairs - 1 - pair, other, :] = back.astype(jnp.bfloat16)
            else:
                total = a.astype(jnp.float32) + turned[pair, here, :].astype(jnp.float32)
                turned[pair, here, :] = total.astype(jnp.bfloat16)
                opposite = columns_of(pairs - 1 - pair)
                total = yf_ref[other, opposite].astype(jnp.float32) + back
                yf_ref[other, opposite] = total.astype(jnp.bfloat16)
            return carry

        lax.fori_loop(0, blocks, block_step, 0)
        if strand == 1:
            send_back(pair).start()

    def attend_all(strand):
        def pair_step(pair, carry):
            attend(strand, pair)
            return carry

        lax.fori_loop(0, pairs, pair_step, 0)

    load_x.wait()
    load_w.wait()
    project(x_own, 0, 0, WINDOW, rows, 0)
    pl.when(has_left)(lambda: to_right().wait_recv())
    pl.when(has_right)(lambda: to_left().wait_recv())
    for chunk in range(chunks):
        cross(chunk).start()
    project_side(0, 0)
    project_side(0, 1)
    attend_all(0)

    per = BLOCK // LANES
    for chunk in range(chunks):
        cross(chunk).wait_recv()
        if chunk in near_left:
            pl.when(pass_left)(lambda: hand_left(chunk).start())
        if chunk in near_right:
            pl.when(pass_right)(lambda: hand_right(chunk).start())
        if chunk % per == per - 1:
            at = (chunk + 1 - per) * LANES
            project(x_own, 1, at, WINDOW + at, BLOCK, 0)

    def wait_low():
        for chunk in near_left:
            pl.when(pass_right)(lambda: hand_left(chunk).wait_recv())
        pl.when(mid_low)(lambda: keep_low.wait())

    def wait_high():
        for chunk in near_right:
            pl.when(pass_left)(lambda: hand_right(chunk).wait_recv())
        pl.when(mid_high)(lambda: keep_high.wait())

    outer = jnp.where(me < count // 2, 1, 0)
    pl.when(me < count // 2)(wait_high)
    pl.when(me >= count // 2)(wait_low)
    project_side(1, outer)
    pl.when(me < count // 2)(wait_low)
    pl.when(me >= count // 2)(wait_high)
    project_side(1, 1 - outer)
    attend_all(1)

    def finish(pair, carry):
        send_back(pair).wait_recv()
        send_back(pair).wait_send()
        return carry

    lax.fori_loop(0, pairs, finish, 0)
    for chunk in range(chunks):
        cross(chunk).wait_send()
        if chunk in near_left:
            pl.when(pass_left)(lambda: hand_left(chunk).wait_send())
        if chunk in near_right:
            pl.when(pass_right)(lambda: hand_right(chunk).wait_send())
    pl.when(has_right)(lambda: to_right().wait_send())
    pl.when(has_left)(lambda: to_left().wait_send())


def per_device(x_fwd, x_rev, gain, w_qkv):
    rows, width = x_fwd.shape
    count = lax.axis_size("seq")
    pairs = width // LANES
    chunks = rows // LANES
    ext = rows + 2 * WINDOW
    scale = (width // HEADS) ** (-0.5) * math.log2(math.e)
    anywhere = pl.BlockSpec(memory_space=pl.ANY)
    inside = pl.BlockSpec(memory_space=pltpu.VMEM)
    half = jnp.bfloat16
    return pl.pallas_call(
        functools.partial(kernel, count, scale),
        in_specs=[inside, anywhere, anywhere, anywhere],
        out_specs=[inside, inside],
        out_shape=[jax.ShapeDtypeStruct((rows, width), half)] * 2,
        scratch_shapes=[
            pltpu.VMEM((2, rows, width), half),
            pltpu.VMEM((2, 2 * WINDOW, width), half),
            pltpu.VMEM((width, 3 * width), half),
            pltpu.VMEM((max(rows, WINDOW), width), half),
            pltpu.VMEM((2, ext, 3 * width), half),
            pltpu.VMEM((2, ext, LANES), half),
            pltpu.VMEM((2, ext, LANES), half),
            pltpu.VMEM((2, ext, LANES), half),
            pltpu.VMEM((2, BLOCK, BLOCK), jnp.float32),
            pltpu.VMEM((BLOCK, BLOCK), half),
            pltpu.VMEM((pairs, rows, LANES), half),
            pltpu.SemaphoreType.DMA((3,)),
            pltpu.SemaphoreType.DMA((2,)),
            pltpu.SemaphoreType.DMA((2,)),
            pltpu.SemaphoreType.DMA((chunks,)),
            pltpu.SemaphoreType.DMA((chunks,)),
            pltpu.SemaphoreType.DMA((2, chunks)),
            pltpu.SemaphoreType.DMA((2, chunks)),
            pltpu.SemaphoreType.DMA((pairs,)),
            pltpu.SemaphoreType.DMA((pairs,)),
        ],
        compiler_params=pltpu.CompilerParams(
            collective_id=0, has_side_effects=True, vmem_limit_bytes=62 * 1024 * 1024
        ),
        cost_estimate=pl.CostEstimate(
            flops=2 * rows * width * 3 * width * 4,
            bytes_accessed=2 * (4 * rows * width + 3 * width * width),
            transcendentals=2 * HEADS * rows * (2 * WINDOW + BLOCK),
        ),
    )(gain.reshape(1, -1), x_fwd, x_rev, w_qkv)


def solution(mesh):
    in_specs = (P(("dp", "seq"), None), P(("dp", "seq"), None), P(), P())
    out_specs = (P(("dp", "seq"), None), P(("dp", "seq"), None))
    return jax.shard_map(
        per_device, mesh=mesh, in_specs=in_specs, out_specs=out_specs, check_vma=False
    )
```

time: 126 us -> 129 us (1.024)
  Pallas kernels: 120 us -> 122 us
  local copies, waits for them, and re-layouts: 4.31 us -> 5.8 us
    unnamed x0 -> x2, local copies, waits for them, and re-layouts: none -> 4.52 us
    squeeze x1 -> x0, local copies, waits for them, and re-layouts: 3.03 us -> none  [per_device(): return (y[0], y[1])]
    pallas_call x1, Pallas kernels: 120 us -> 122 us  [per_device(): pl.pallas_call(functools.partial(kernel, count, scale), in_specs=[inside,...]
where the time goes in v3:
time: 129 us
  Pallas kernels  122 us (95%)
  local copies, waits for them, and re-layouts  5.8 us (4%)
    pallas_call x1, Pallas kernels, per_device(): pl.pallas_call(functools.partial(kernel, count, scale), in_specs=[inside,...  122 us
    unnamed x2, local copies, waits for them, and re-layouts  4.52 us

profile of v3, /device:TPU:12, one launch (start us, length us, event | category | flops | bytes accessed | tf_op | source)
XLA Modules:
  0.0 128.7 jit_solution(14488830261864637408)
XLA Ops:
  0.6 1.3 reshape.7.gain_ref
  1.9 122.2 %shard_map.59 = (bf16[512,1024]{1,0:T(8,128)(2,1)}, bf16[512,1024]{1,0:T(8,128)(2,1)}) custom-call(bf16[1,1024]{1,0:T(2,128)(2,1)} %reshape.7.gain_ref, bf16[512,1024]{1,0:T(8,128)(2,1)} %xf_ref.1, bf16[512,1024]{1,0:T(8,128)(2,1)} %xr_ref.1, bf16[1024,3072]{1,0:T(8,128)(2,1)} %w_ref.1), custom_call_target="tpu_custom_call" | custom-call | flops 12884901888 | bytes 10485760 | tf_op jit(solution)/shard_map/pallas_call | solution.py:307
  124.2 2.3 %copy.8 = bf16[512,1024]{1,0:T(8,128)(2,1)} copy(bf16[512,1024]{1,0:T(8,128)(2,1)} %get-tuple-element.4) | data formatting | bytes 2097152
  126.4 2.3 %copy.9 = bf16[512,1024]{1,0:T(8,128)(2,1)} copy(bf16[512,1024]{1,0:T(8,128)(2,1)} %get-tuple-element.5) | data formatting | bytes 2097152

commit v4 on v3

--- a/solution.py
+++ b/solution.py
@@ -18,8 +18,8 @@
 
 
 def kernel(
-    count, scale, gain_ref, xf_ref, xr_ref, w_ref, yf_ref, yr_ref,
-    x_own, x_halo, w_vmem, hn, qkv, kx, vx, bias, band, flip, turned,
+    count, scale, gain_ref, xf_ref, xr_ref, w_ref, y_ref,
+    x_own, x_halo, w_vmem, hn, qkv, qkv_group, kx, vx, bias, band, flip, turned,
     load_sem, halo_send, halo_recv, cross_send, cross_recv, pass_send, pass_recv, back_send, back_recv,
 ):
     rows = xf_ref.shape[0]
@@ -105,7 +105,7 @@
 
     def send_back(pair):
         return remote(
-            turned.at[pair], yr_ref.at[:, columns_of(pair)],
+            turned.at[pair], y_ref.at[1, :, columns_of(pair)],
             back_send.at[pair], back_recv.at[pair], across,
         )
 
@@ -129,86 +129,107 @@
     band[0] = jnp.where(col >= row, 0.0, FAR)
     band[1] = jnp.where(col <= row, 0.0, FAR)
     flip[...] = jnp.where(col + row == BLOCK - 1, 1.0, 0.0).astype(jnp.bfloat16)
-    key = lax.broadcasted_iota(jnp.int32, (ext, LANES), 0)
+    key = lax.broadcasted_iota(jnp.int32, (LANES, ext), 1)
     for strand, (before, after) in enumerate(((has_left, has_right), (has_right, has_left))):
         first = jnp.where(before, 0, WINDOW)
         last = jnp.where(after, ext, WINDOW + rows)
         bias[strand] = jnp.where((key >= first) & (key < last), 0.0, FAR).astype(jnp.bfloat16)
 
-    def project(source, strand, src, dst, total, first_tile):
-        def normalise(i, carry):
+    def normalise(source, strand, src, dst, total):
+        def step(i, carry):
             at = pl.ds(pl.multiple_of(src + i * LANES, LANES), LANES)
             xf = source[strand, at, :].astype(jnp.float32)
             meansq = jnp.mean(xf * xf, axis=-1, keepdims=True)
             out = xf * lax.rsqrt(meansq + 1e-06) * gain_ref[...].astype(jnp.float32)
-            hn[pl.ds(pl.multiple_of(i * LANES, LANES), LANES), :] = out.astype(jnp.bfloat16)
-            return carry
-
-        lax.fori_loop(0, total // LANES, normalise, 0)
-
-        def step(j, carry):
-            at = pl.ds(pl.multiple_of(j * TILE, TILE), TILE)
-            out = jnp.dot(hn[:total, :], w_vmem[:, at], preferred_element_type=jnp.float32)
-            out = out * jnp.where(j < width // TILE, scale, 1.0)
-            qkv[strand, pl.ds(pl.multiple_of(dst, LANES), total), at] = out.astype(jnp.bfloat16)
-            return carry
-
-        lax.fori_loop(first_tile, 3 * width // TILE, step, 0)
-
-    def project_side(strand, side):
-        project(x_halo, strand, side * WINDOW, side * (WINDOW + rows), WINDOW, width // TILE)
+            hn[pl.ds(pl.multiple_of(dst + i * LANES, LANES), LANES), :] = out.astype(jnp.bfloat16)
+            return carry
+
+        lax.fori_loop(0, total // LANES, step, 0)
+
+    tiles = width // TILE
+    middle, ends = (WINDOW, rows), ((0, WINDOW), (WINDOW + rows, WINDOW))
+
+    def project(out_ref, span_rows, tile, to):
+        start, size = span_rows
+        at = pl.ds(pl.multiple_of(tile * TILE, TILE), TILE)
+        out = jnp.dot(hn[start:start + size, :], w_vmem[:, at], preferred_element_type=jnp.float32)
+        out = out * jnp.where(tile < tiles, scale, 1.0)
+        to = pl.ds(pl.multiple_of(to * TILE, TILE), TILE)
+        out_ref[start:start + size, to] = out.astype(jnp.bfloat16)
+
+    def project_fwd(span_rows, first_tile):
+        def step(tile, carry):
+            project(qkv, span_rows, tile, tile)
+            return carry
+
+        lax.fori_loop(first_tile, 3 * tiles, step, 0)
+
+    def project_group(group):
+        def own(part, carry):
+            project(qkv_group, middle, part * tiles + group, part)
+            return carry
+
+        def halo(part, carry):
+            for end in ends:
+                project(qkv_group, end, part * tiles + group, part)
+            return carry
+
+        lax.fori_loop(0, 3, own, 0)
+        lax.fori_loop(1, 3, halo, 0)
 
     lane = lax.broadcasted_iota(jnp.int32, (BLOCK, LANES), 1)
     low = lane < LANES // 2
 
+    high_rows = lax.broadcasted_iota(jnp.int32, (LANES, BLOCK), 0) < LANES // 2
+
     def attend(strand, pair):
-        columns = [columns_of(pair + part * pairs) for part in range(3)]
+        if strand == 0:
+            source, columns = qkv, [columns_of(pair + part * pairs) for part in range(3)]
+        else:
+            per = TILE // LANES
+            source, columns = qkv_group, [columns_of(pair % per + part * per) for part in range(3)]
+        own_columns = columns_of(pair)
 
         def lay(i, carry):
             at = pl.ds(pl.multiple_of(i * BLOCK, BLOCK), BLOCK)
-            k = qkv[strand, at, columns[1]]
-            v = qkv[strand, at, columns[2]]
-            side = bias[strand, at, :]
+            k = source[at, columns[1]].T
+            v = source[at, columns[2]]
+            side = bias[strand, :, at]
             one = jnp.ones_like(v)
-            kx[0, at, :] = jnp.where(low, k, side)
-            kx[1, at, :] = jnp.where(low, side, k)
+            kx[0, :, at] = jnp.where(high_rows, k, side)
+            kx[1, :, at] = jnp.where(high_rows, side, k)
             vx[0, at, :] = jnp.where(low, v, one)
             vx[1, at, :] = jnp.where(low, one, v)
             return carry
 
         lax.fori_loop(0, ext // BLOCK, lay, 0)
-
-        def block_step(block, carry):
-            start = pl.multiple_of(block * BLOCK, BLOCK)
+        cuts = ((0, BLOCK), (BLOCK, 2 * WINDOW - BLOCK), (2 * WINDOW, BLOCK))
+
+        def score(start, head):
+            q = source[pl.ds(pl.multiple_of(WINDOW + start, BLOCK), BLOCK), columns[0]]
+            mark = jnp.where(lane == (LANES // 2 if head == 0 else 0), 1.0, 0.0).astype(jnp.bfloat16)
+            qh = jnp.where(low if head == 0 else jnp.logical_not(low), q, mark)
+            return [
+                jnp.dot(
+                    qh, kx[head, :, pl.ds(pl.multiple_of(start + offset, BLOCK), size)],
+                    preferred_element_type=jnp.float32,
+                )
+                for offset, size in cuts
+            ]
+
+        def weigh(start, head, scores):
+            one, two, three = scores
+            one = one + band[0]
+            three = three + band[1]
+            top = jnp.max(two, axis=-1, keepdims=True)
+            top = jnp.maximum(top, jnp.max(jnp.maximum(one, three), axis=-1, keepdims=True))
+            p = jnp.concatenate(
+                [jnp.exp2(s - top).astype(jnp.bfloat16) for s in (one, two, three)], axis=1
+            )
+            return jnp.dot(p, vx[head, pl.ds(start, span), :], preferred_element_type=jnp.float32)
+
+        def store(block, start, outs):
             here = pl.ds(start, BLOCK)
-            q = qkv[strand, pl.ds(pl.multiple_of(WINDOW + start, BLOCK), BLOCK), columns[0]]
-            cuts = ((0, BLOCK), (BLOCK, 2 * WINDOW - BLOCK), (2 * WINDOW, BLOCK))
-            scores = []
-            for head in range(2):
-                mark = jnp.where(lane == (LANES // 2 if head == 0 else 0), 1.0, 0.0).astype(jnp.bfloat16)
-                qh = jnp.where(low if head == 0 else jnp.logical_not(low), q, mark)
-                scores.append(
-                    [
-                        lax.dot_general(
-                            qh, kx[head, pl.ds(pl.multiple_of(start + offset, BLOCK), size), :],
-                            (((1,), (1,)), ((), ())), preferred_element_type=jnp.float32,
-                        )
-                        for offset, size in cuts
-                    ]
-                )
-            outs = []
-            for head in range(2):
-                one, two, three = scores[head]
-                one = one + band[0]
-                three = three + band[1]
-                top = jnp.max(two, axis=-1, keepdims=True)
-                top = jnp.maximum(top, jnp.max(jnp.maximum(one, three), axis=-1, keepdims=True))
-                p = jnp.concatenate(
-                    [jnp.exp2(s - top).astype(jnp.bfloat16) for s in (one, two, three)], axis=1
-                )
-                outs.append(
-                    jnp.dot(p, vx[head, pl.ds(start, span), :], preferred_element_type=jnp.float32)
-                )
             num = jnp.where(low, outs[0], outs[1])
             den = pltpu.roll(jnp.where(low, outs[1], outs[0]), LANES // 2, 1)
             a = (num / den).astype(jnp.bfloat16)
@@ -216,48 +237,61 @@
             back = jnp.dot(back, flip[:LANES, BLOCK - LANES:], preferred_element_type=jnp.float32)
             other = pl.ds(pl.multiple_of((blocks - 1 - block) * BLOCK, BLOCK), BLOCK)
             if strand == 0:
-                yf_ref[here, columns[0]] = a
+                y_ref[0, here, own_columns] = a
                 turned[pairs - 1 - pair, other, :] = back.astype(jnp.bfloat16)
             else:
                 total = a.astype(jnp.float32) + turned[pair, here, :].astype(jnp.float32)
                 turned[pair, here, :] = total.astype(jnp.bfloat16)
                 opposite = columns_of(pairs - 1 - pair)
-                total = yf_ref[other, opposite].astype(jnp.float32) + back
-                yf_ref[other, opposite] = total.astype(jnp.bfloat16)
-            return carry
-
-        lax.fori_loop(0, blocks, block_step, 0)
+                total = y_ref[0, other, opposite].astype(jnp.float32) + back
+                y_ref[0, other, opposite] = total.astype(jnp.bfloat16)
+
+        def blocks_step(step, carry):
+            units = [
+                (2 * step + sub, pl.multiple_of((2 * step + sub) * BLOCK, BLOCK), head)
+                for sub in range(2) for head in range(2)
+            ]
+            ahead = score(*units[0][1:])
+            outs = []
+            for i, (block, start, head) in enumerate(units):
+                scores = ahead
+                if i + 1 < len(units):
+                    ahead = score(*units[i + 1][1:])
+                outs.append(weigh(start, head, scores))
+                if head == 1:
+                    store(block, start, outs[-2:])
+            return carry
+
+        lax.fori_loop(0, blocks // 2, blocks_step, 0)
         if strand == 1:
             send_back(pair).start()
 
-    def attend_all(strand):
-        def pair_step(pair, carry):
-            attend(strand, pair)
-            return carry
-
-        lax.fori_loop(0, pairs, pair_step, 0)
-
     load_x.wait()
     load_w.wait()
-    project(x_own, 0, 0, WINDOW, rows, 0)
+    normalise(x_own, 0, 0, WINDOW, rows)
+    project_fwd(middle, 0)
     pl.when(has_left)(lambda: to_right().wait_recv())
     pl.when(has_right)(lambda: to_left().wait_recv())
     for chunk in range(chunks):
         cross(chunk).start()
-    project_side(0, 0)
-    project_side(0, 1)
-    attend_all(0)
-
-    per = BLOCK // LANES
+    normalise(x_halo, 0, 0, 0, WINDOW)
+    normalise(x_halo, 0, WINDOW, WINDOW + rows, WINDOW)
+    for end in ends:
+        project_fwd(end, tiles)
+
+    def fwd_step(pair, carry):
+        attend(0, pair)
+        return carry
+
+    lax.fori_loop(0, pairs, fwd_step, 0)
+
     for chunk in range(chunks):
         cross(chunk).wait_recv()
         if chunk in near_left:
             pl.when(pass_left)(lambda: hand_left(chunk).start())
         if chunk in near_right:
             pl.when(pass_right)(lambda: hand_right(chunk).start())
-        if chunk % per == per - 1:
-            at = (chunk + 1 - per) * LANES
-            project(x_own, 1, at, WINDOW + at, BLOCK, 0)
+        normalise(x_own, 1, chunk * LANES, WINDOW + chunk * LANES, LANES)
 
     def wait_low():
         for chunk in near_left:
@@ -270,13 +304,20 @@
         pl.when(mid_high)(lambda: keep_high.wait())
 
     outer = jnp.where(me < count // 2, 1, 0)
+    inner = 1 - outer
     pl.when(me < count // 2)(wait_high)
     pl.when(me >= count // 2)(wait_low)
-    project_side(1, outer)
+    normalise(x_halo, 1, outer * WINDOW, outer * (WINDOW + rows), WINDOW)
     pl.when(me < count // 2)(wait_low)
     pl.when(me >= count // 2)(wait_high)
-    project_side(1, 1 - outer)
-    attend_all(1)
+    normalise(x_halo, 1, inner * WINDOW, inner * (WINDOW + rows), WINDOW)
+
+    def rev_step(pair, carry):
+        pl.when(pair % (TILE // LANES) == 0)(lambda: project_group(pair // (TILE // LANES)))
+        attend(1, pair)
+        return carry
+
+    lax.fori_loop(0, pairs, rev_step, 0)
 
     def finish(pair, carry):
         send_back(pair).wait_recv()
@@ -304,20 +345,21 @@
     anywhere = pl.BlockSpec(memory_space=pl.ANY)
     inside = pl.BlockSpec(memory_space=pltpu.VMEM)
     half = jnp.bfloat16
-    return pl.pallas_call(
+    y = pl.pallas_call(
         functools.partial(kernel, count, scale),
         in_specs=[inside, anywhere, anywhere, anywhere],
-        out_specs=[inside, inside],
-        out_shape=[jax.ShapeDtypeStruct((rows, width), half)] * 2,
+        out_specs=inside,
+        out_shape=jax.ShapeDtypeStruct((2, rows, width), half),
         scratch_shapes=[
             pltpu.VMEM((2, rows, width), half),
             pltpu.VMEM((2, 2 * WINDOW, width), half),
             pltpu.VMEM((width, 3 * width), half),
-            pltpu.VMEM((max(rows, WINDOW), width), half),
-            pltpu.VMEM((2, ext, 3 * width), half),
+            pltpu.VMEM((ext, width), half),
+            pltpu.VMEM((ext, 3 * width), half),
+            pltpu.VMEM((ext, 3 * TILE), half),
+            pltpu.VMEM((2, LANES, ext), half),
             pltpu.VMEM((2, ext, LANES), half),
-            pltpu.VMEM((2, ext, LANES), half),
-            pltpu.VMEM((2, ext, LANES), half),
+            pltpu.VMEM((2, LANES, ext), half),
             pltpu.VMEM((2, BLOCK, BLOCK), jnp.float32),
             pltpu.VMEM((BLOCK, BLOCK), half),
             pltpu.VMEM((pairs, rows, LANES), half),
@@ -339,7 +381,8 @@
             bytes_accessed=2 * (4 * rows * width + 3 * width * width),
             transcendentals=2 * HEADS * rows * (2 * WINDOW + BLOCK),
         ),
-    )(gain.reshape(1, -1), x_fwd, x_rev, w_qkv)
+    )(gain, x_fwd, x_rev, w_qkv)
+    return y[0], y[1]
 
 
 def solution(mesh):

time: 129 us -> 124 us (0.961)
  Pallas kernels: 122 us -> 119 us
  local copies, waits for them, and re-layouts: 5.8 us -> 3.03 us
    unnamed x2 -> x0, local copies, waits for them, and re-layouts: 4.52 us -> none
    squeeze x0 -> x1, local copies, waits for them, and re-layouts: none -> 3.03 us  [per_device(): return (y[0], y[1])]
    pallas_call x1, Pallas kernels: 122 us -> 119 us  [per_device(): pl.pallas_call(functools.partial(kernel, count, scale), in_specs=[inside,...]
where the time goes in v4:
time: 124 us; the launch traced here: 123 us
  Pallas kernels  119 us (96%)
  local copies, waits for them, and re-layouts  3.03 us (2%)
    pallas_call x1, Pallas kernels, per_device(): pl.pallas_call(functools.partial(kernel, count, scale), in_specs=[inside,...  119 us
    squeeze x1, local copies, waits for them, and re-layouts, per_device(): return (y[0], y[1])  3.03 us

profile of v4, /device:TPU:12, one launch (start us, length us, event | category | flops | bytes accessed | tf_op | source)
XLA Modules:
  0.0 122.9 jit_solution(11769308627009415690)
XLA Ops:
  0.6 119.3 %shard_map.59 = bf16[2,512,1024]{2,1,0:T(8,128)(2,1)} custom-call(bf16[1024]{0:T(1024)(128)(2,1)} %gain_ref.1, bf16[512,1024]{1,0:T(8,128)(2,1)} %xf_ref.1, bf16[512,1024]{1,0:T(8,128)(2,1)} %xr_ref.1, bf16[1024,3072]{1,0:T(8,128)(2,1)} %w_ref.1), custom_call_target="tpu_custom_call" | custom-call | flops 12884901888 | bytes 10485760 | tf_op jit(solution)/shard_map/pallas_call | solution.py:348
  119.9 3.0 %slice_bitcast_fusion = (bf16[512,1024]{1,0:T(8,128)(2,1)}, bf16[512,1024]{1,0:T(8,128)(2,1)}) fusion(bf16[2,512,1024]{2,1,0:T(8,128)(2,1)} %shard_map.59), kind=kLoop, calls=%fused_computation | loop fusion | bytes 4194304 | tf_op jit(solution)/shard_map/squeeze | solution.py:385

commit v5 on v4

--- a/solution.py
+++ b/solution.py
@@ -19,7 +19,7 @@
 
 def kernel(
     count, scale, gain_ref, xf_ref, xr_ref, w_ref, y_ref,
-    x_own, x_halo, w_vmem, hn, qkv, qkv_group, kx, vx, bias, band, flip, turned,
+    x_own, x_halo, w_vmem, hn, qkv, kx, vx, bias, band, flip, turned,
     load_sem, halo_send, halo_recv, cross_send, cross_recv, pass_send, pass_recv, back_send, back_recv,
 ):
     rows = xf_ref.shape[0]
@@ -147,35 +147,28 @@
         lax.fori_loop(0, total // LANES, step, 0)
 
     tiles = width // TILE
-    middle, ends = (WINDOW, rows), ((0, WINDOW), (WINDOW + rows, WINDOW))
-
-    def project(out_ref, span_rows, tile, to):
-        start, size = span_rows
+    ends = ((0, WINDOW), (WINDOW + rows, WINDOW))
+
+    def project(start, size, tile):
         at = pl.ds(pl.multiple_of(tile * TILE, TILE), TILE)
-        out = jnp.dot(hn[start:start + size, :], w_vmem[:, at], preferred_element_type=jnp.float32)
+        here = pl.ds(pl.multiple_of(start, WINDOW), size)
+        out = jnp.dot(hn[here, :], w_vmem[:, at], preferred_element_type=jnp.float32)
         out = out * jnp.where(tile < tiles, scale, 1.0)
-        to = pl.ds(pl.multiple_of(to * TILE, TILE), TILE)
-        out_ref[start:start + size, to] = out.astype(jnp.bfloat16)
-
-    def project_fwd(span_rows, first_tile):
+        qkv[here, at] = out.astype(jnp.bfloat16)
+
+    def project_all(start, size, first_tile):
         def step(tile, carry):
-            project(qkv, span_rows, tile, tile)
+            project(start, size, tile)
             return carry
 
         lax.fori_loop(first_tile, 3 * tiles, step, 0)
 
-    def project_group(group):
-        def own(part, carry):
-            project(qkv_group, middle, part * tiles + group, part)
+    def project_group(start, size, first_part, group):
+        def step(part, carry):
+            project(start, size, part * tiles + group)
             return carry
 
-        def halo(part, carry):
-            for end in ends:
-                project(qkv_group, end, part * tiles + group, part)
-            return carry
-
-        lax.fori_loop(0, 3, own, 0)
-        lax.fori_loop(1, 3, halo, 0)
+        lax.fori_loop(first_part, 3, step, 0)
 
     lane = lax.broadcasted_iota(jnp.int32, (BLOCK, LANES), 1)
     low = lane < LANES // 2
@@ -183,17 +176,13 @@
     high_rows = lax.broadcasted_iota(jnp.int32, (LANES, BLOCK), 0) < LANES // 2
 
     def attend(strand, pair):
-        if strand == 0:
-            source, columns = qkv, [columns_of(pair + part * pairs) for part in range(3)]
-        else:
-            per = TILE // LANES
-            source, columns = qkv_group, [columns_of(pair % per + part * per) for part in range(3)]
+        columns = [columns_of(pair + part * pairs) for part in range(3)]
         own_columns = columns_of(pair)
 
         def lay(i, carry):
             at = pl.ds(pl.multiple_of(i * BLOCK, BLOCK), BLOCK)
-            k = source[at, columns[1]].T
-            v = source[at, columns[2]]
+            k = qkv[at, columns[1]].T
+            v = qkv[at, columns[2]]
             side = bias[strand, :, at]
             one = jnp.ones_like(v)
             kx[0, :, at] = jnp.where(high_rows, k, side)
@@ -206,7 +195,7 @@
         cuts = ((0, BLOCK), (BLOCK, 2 * WINDOW - BLOCK), (2 * WINDOW, BLOCK))
 
         def score(start, head):
-            q = source[pl.ds(pl.multiple_of(WINDOW + start, BLOCK), BLOCK), columns[0]]
+            q = qkv[pl.ds(pl.multiple_of(WINDOW + start, BLOCK), BLOCK), columns[0]]
             mark = jnp.where(lane == (LANES // 2 if head == 0 else 0), 1.0, 0.0).astype(jnp.bfloat16)
             qh = jnp.where(low if head == 0 else jnp.logical_not(low), q, mark)
             return [
@@ -269,21 +258,36 @@
     load_x.wait()
     load_w.wait()
     normalise(x_own, 0, 0, WINDOW, rows)
-    project_fwd(middle, 0)
+    project_all(WINDOW, rows, 0)
     pl.when(has_left)(lambda: to_right().wait_recv())
     pl.when(has_right)(lambda: to_left().wait_recv())
     for chunk in range(chunks):
         cross(chunk).start()
     normalise(x_halo, 0, 0, 0, WINDOW)
     normalise(x_halo, 0, WINDOW, WINDOW + rows, WINDOW)
-    for end in ends:
-        project_fwd(end, tiles)
+    for end, size in ends:
+        project_all(end, size, tiles)
 
     def fwd_step(pair, carry):
         attend(0, pair)
         return carry
 
     lax.fori_loop(0, pairs, fwd_step, 0)
+
+    outer = jnp.where(me < count // 2, 1, 0)
+    inner = 1 - outer
+    outer_start, inner_start = outer * (WINDOW + rows), inner * (WINDOW + rows)
+    middle = mid_low | mid_high
+    edge = no_left | no_right
+    early = ((me < count // 4) | (me >= count - count // 4)) & jnp.logical_not(edge)
+
+    pl.when(mid_low)(lambda: keep_low.wait())
+    pl.when(mid_high)(lambda: keep_high.wait())
+
+    @pl.when(middle)
+    def _():
+        normalise(x_halo, 1, inner * WINDOW, inner_start, WINDOW)
+        project_all(inner_start, WINDOW, tiles)
 
     for chunk in range(chunks):
         cross(chunk).wait_recv()
@@ -296,24 +300,34 @@
     def wait_low():
         for chunk in near_left:
             pl.when(pass_right)(lambda: hand_left(chunk).wait_recv())
-        pl.when(mid_low)(lambda: keep_low.wait())
 
     def wait_high():
         for chunk in near_right:
             pl.when(pass_left)(lambda: hand_right(chunk).wait_recv())
-        pl.when(mid_high)(lambda: keep_high.wait())
-
-    outer = jnp.where(me < count // 2, 1, 0)
-    inner = 1 - outer
+
+    pl.when(early)(lambda: project_all(WINDOW, rows, 0))
     pl.when(me < count // 2)(wait_high)
     pl.when(me >= count // 2)(wait_low)
-    normalise(x_halo, 1, outer * WINDOW, outer * (WINDOW + rows), WINDOW)
+
+    @pl.when(jnp.logical_not(edge))
+    def _():
+        normalise(x_halo, 1, outer * WINDOW, outer_start, WINDOW)
+
+    pl.when(early)(lambda: project_all(outer_start, WINDOW, tiles))
     pl.when(me < count // 2)(wait_low)
     pl.when(me >= count // 2)(wait_high)
-    normalise(x_halo, 1, inner * WINDOW, inner * (WINDOW + rows), WINDOW)
+
+    @pl.when(jnp.logical_not(middle))
+    def _():
+        normalise(x_halo, 1, inner * WINDOW, inner_start, WINDOW)
+
+    def prepare(group):
+        pl.when(jnp.logical_not(early))(lambda: project_group(WINDOW, rows, 0, group))
+        pl.when(jnp.logical_not(early | edge))(lambda: project_group(outer_start, WINDOW, 1, group))
+        pl.when(jnp.logical_not(middle))(lambda: project_group(inner_start, WINDOW, 1, group))
 
     def rev_step(pair, carry):
-        pl.when(pair % (TILE // LANES) == 0)(lambda: project_group(pair // (TILE // LANES)))
+        pl.when(pair % (TILE // LANES) == 0)(lambda: prepare(pair // (TILE // LANES)))
         attend(1, pair)
         return carry
 
@@ -356,7 +370,6 @@
             pltpu.VMEM((width, 3 * width), half),
             pltpu.VMEM((ext, width), half),
             pltpu.VMEM((ext, 3 * width), half),
-            pltpu.VMEM((ext, 3 * TILE), half),
             pltpu.VMEM((2, LANES, ext), half),
             pltpu.VMEM((2, ext, LANES), half),
             pltpu.VMEM((2, LANES, ext), half),

time: 124 us -> 123 us (level)
  no operation moved by 1% of the time
where the time goes in v5:
time: 123 us
  Pallas kernels  119 us (97%)
  local copies, waits for them, and re-layouts  3.03 us (2%)
    pallas_call x1, Pallas kernels, per_device(): pl.pallas_call(functools.partial(kernel, count, scale), in_specs=[inside,...  119 us
    squeeze x1, local copies, waits for them, and re-layouts, per_device(): return (y[0], y[1])  3.03 us

profile of v5, /device:TPU:12, one launch (start us, length us, event | category | flops | bytes accessed | tf_op | source)
XLA Modules:
  0.0 122.8 jit_solution(5051977942073171929)
XLA Ops:
  0.6 119.1 %shard_map.59 = bf16[2,512,1024]{2,1,0:T(8,128)(2,1)} custom-call(bf16[1024]{0:T(1024)(128)(2,1)} %gain_ref.1, bf16[512,1024]{1,0:T(8,128)(2,1)} %xf_ref.1, bf16[512,1024]{1,0:T(8,128)(2,1)} %xr_ref.1, bf16[1024,3072]{1,0:T(8,128)(2,1)} %w_ref.1), custom_call_target="tpu_custom_call" | custom-call | flops 12884901888 | bytes 10485760 | tf_op jit(solution)/shard_map/pallas_call | solution.py:362
  119.8 3.0 %slice_bitcast_fusion = (bf16[512,1024]{1,0:T(8,128)(2,1)}, bf16[512,1024]{1,0:T(8,128)(2,1)}) fusion(bf16[2,512,1024]{2,1,0:T(8,128)(2,1)} %shard_map.59), kind=kLoop, calls=%fused_computation | loop fusion | bytes 4194304 | tf_op jit(solution)/shard_map/squeeze | solution.py:398

commit v6 on v5

--- a/solution.py
+++ b/solution.py
@@ -151,7 +151,7 @@
 
     def project(start, size, tile):
         at = pl.ds(pl.multiple_of(tile * TILE, TILE), TILE)
-        here = pl.ds(pl.multiple_of(start, WINDOW), size)
+        here = pl.ds(pl.multiple_of(start, BLOCK), size)
         out = jnp.dot(hn[here, :], w_vmem[:, at], preferred_element_type=jnp.float32)
         out = out * jnp.where(tile < tiles, scale, 1.0)
         qkv[here, at] = out.astype(jnp.bfloat16)
@@ -179,8 +179,8 @@
         columns = [columns_of(pair + part * pairs) for part in range(3)]
         own_columns = columns_of(pair)
 
-        def lay(i, carry):
-            at = pl.ds(pl.multiple_of(i * BLOCK, BLOCK), BLOCK)
+        for i in range(ext // BLOCK):
+            at = pl.ds(i * BLOCK, BLOCK)
             k = qkv[at, columns[1]].T
             v = qkv[at, columns[2]]
             side = bias[strand, :, at]
@@ -189,9 +189,7 @@
             kx[1, :, at] = jnp.where(high_rows, side, k)
             vx[0, at, :] = jnp.where(low, v, one)
             vx[1, at, :] = jnp.where(low, one, v)
-            return carry
-
-        lax.fori_loop(0, ext // BLOCK, lay, 0)
+
         cuts = ((0, BLOCK), (BLOCK, 2 * WINDOW - BLOCK), (2 * WINDOW, BLOCK))
 
         def score(start, head):
@@ -217,43 +215,59 @@
             )
             return jnp.dot(p, vx[head, pl.ds(start, span), :], preferred_element_type=jnp.float32)
 
-        def store(block, start, outs):
+        def store(start, outs):
             here = pl.ds(start, BLOCK)
             num = jnp.where(low, outs[0], outs[1])
             den = pltpu.roll(jnp.where(low, outs[1], outs[0]), LANES // 2, 1)
             a = (num / den).astype(jnp.bfloat16)
-            back = jnp.dot(flip[...], a, preferred_element_type=jnp.float32).astype(jnp.bfloat16)
-            back = jnp.dot(back, flip[:LANES, BLOCK - LANES:], preferred_element_type=jnp.float32)
-            other = pl.ds(pl.multiple_of((blocks - 1 - block) * BLOCK, BLOCK), BLOCK)
             if strand == 0:
                 y_ref[0, here, own_columns] = a
-                turned[pairs - 1 - pair, other, :] = back.astype(jnp.bfloat16)
             else:
+                x_own[0, here, own_columns] = a
                 total = a.astype(jnp.float32) + turned[pair, here, :].astype(jnp.float32)
                 turned[pair, here, :] = total.astype(jnp.bfloat16)
-                opposite = columns_of(pairs - 1 - pair)
-                total = y_ref[0, other, opposite].astype(jnp.float32) + back
-                y_ref[0, other, opposite] = total.astype(jnp.bfloat16)
 
         def blocks_step(step, carry):
             units = [
-                (2 * step + sub, pl.multiple_of((2 * step + sub) * BLOCK, BLOCK), head)
+                (pl.multiple_of((2 * step + sub) * BLOCK, BLOCK), head)
                 for sub in range(2) for head in range(2)
             ]
-            ahead = score(*units[0][1:])
+            ahead = score(*units[0])
             outs = []
-            for i, (block, start, head) in enumerate(units):
+            for i, (start, head) in enumerate(units):
                 scores = ahead
                 if i + 1 < len(units):
-                    ahead = score(*units[i + 1][1:])
+                    ahead = score(*units[i + 1])
                 outs.append(weigh(start, head, scores))
                 if head == 1:
-                    store(block, start, outs[-2:])
+                    store(start, outs[-2:])
             return carry
 
-        lax.fori_loop(0, blocks // 2, blocks_step, 0)
+        if blocks == 2:
+            blocks_step(0, 0)
+        else:
+            lax.fori_loop(0, blocks // 2, blocks_step, 0)
         if strand == 1:
             send_back(pair).start()
+
+    def reverse(source_ref, take):
+        for group in range(tiles):
+            for block in range(blocks):
+                a = source_ref[0, block * BLOCK:(block + 1) * BLOCK, group * TILE:(group + 1) * TILE]
+                back = jnp.dot(flip[...], a, preferred_element_type=jnp.float32).astype(jnp.bfloat16)
+                back = jnp.dot(back, flip[...], preferred_element_type=jnp.float32)
+                other = (blocks - 1 - block) * BLOCK
+                take(slice(other, other + BLOCK), tiles - 1 - group, back)
+
+    def keep_turned(at, group, back):
+        per = TILE // LANES
+        for part in range(per):
+            piece = back[:, part * LANES:(part + 1) * LANES]
+            turned[group * per + part, at, :] = piece.astype(jnp.bfloat16)
+
+    def add_turned(at, group, back):
+        cols = slice(group * TILE, (group + 1) * TILE)
+        y_ref[0, at, cols] = (y_ref[0, at, cols].astype(jnp.float32) + back).astype(jnp.bfloat16)
 
     load_x.wait()
     load_w.wait()
@@ -273,6 +287,7 @@
         return carry
 
     lax.fori_loop(0, pairs, fwd_step, 0)
+    reverse(y_ref, keep_turned)
 
     outer = jnp.where(me < count // 2, 1, 0)
     inner = 1 - outer
@@ -296,6 +311,8 @@
         if chunk in near_right:
             pl.when(pass_right)(lambda: hand_right(chunk).start())
         normalise(x_own, 1, chunk * LANES, WINDOW + chunk * LANES, LANES)
+        if chunk == chunks // 2 - 1:
+            project_all(WINDOW, rows // 2, 0)
 
     def wait_low():
         for chunk in near_left:
@@ -305,7 +322,7 @@
         for chunk in near_right:
             pl.when(pass_left)(lambda: hand_right(chunk).wait_recv())
 
-    pl.when(early)(lambda: project_all(WINDOW, rows, 0))
+    pl.when(early)(lambda: project_all(WINDOW + rows // 2, rows // 2, 0))
     pl.when(me < count // 2)(wait_high)
     pl.when(me >= count // 2)(wait_low)
 
@@ -322,7 +339,7 @@
         normalise(x_halo, 1, inner * WINDOW, inner_start, WINDOW)
 
     def prepare(group):
-        pl.when(jnp.logical_not(early))(lambda: project_group(WINDOW, rows, 0, group))
+        pl.when(jnp.logical_not(early))(lambda: project_group(WINDOW + rows // 2, rows // 2, 0, group))
         pl.when(jnp.logical_not(early | edge))(lambda: project_group(outer_start, WINDOW, 1, group))
         pl.when(jnp.logical_not(middle))(lambda: project_group(inner_start, WINDOW, 1, group))
 
@@ -332,6 +349,7 @@
         return carry
 
     lax.fori_loop(0, pairs, rev_step, 0)
+    reverse(x_own, add_turned)
 
     def finish(pair, carry):
         send_back(pair).wait_recv()

time: 123 us -> 117 us (0.951)
  Pallas kernels: 119 us -> 113 us
    pallas_call x1, Pallas kernels: 119 us -> 113 us  [per_device(): pl.pallas_call(functools.partial(kernel, count, scale), in_specs=[inside,...]
where the time goes in v6:
time: 117 us
  Pallas kernels  113 us (97%)
  local copies, waits for them, and re-layouts  3.03 us (3%)
    pallas_call x1, Pallas kernels, per_device(): pl.pallas_call(functools.partial(kernel, count, scale), in_specs=[inside,...  113 us
    squeeze x1, local copies, waits for them, and re-layouts, per_device(): return (y[0], y[1])  3.03 us

profile of v6, /device:TPU:12, one launch (start us, length us, event | category | flops | bytes accessed | tf_op | source)
XLA Modules:
  0.0 117.0 jit_solution(4628371465493039835)
XLA Ops:
  0.6 113.4 %shard_map.59 = bf16[2,512,1024]{2,1,0:T(8,128)(2,1)} custom-call(bf16[1024]{0:T(1024)(128)(2,1)} %gain_ref.1, bf16[512,1024]{1,0:T(8,128)(2,1)} %xf_ref.1, bf16[512,1024]{1,0:T(8,128)(2,1)} %xr_ref.1, bf16[1024,3072]{1,0:T(8,128)(2,1)} %w_ref.1), custom_call_target="tpu_custom_call" | custom-call | flops 12884901888 | bytes 10485760 | tf_op jit(solution)/shard_map/pallas_call | solution.py:380
  114.0 3.0 %slice_bitcast_fusion = (bf16[512,1024]{1,0:T(8,128)(2,1)}, bf16[512,1024]{1,0:T(8,128)(2,1)}) fusion(bf16[2,512,1024]{2,1,0:T(8,128)(2,1)} %shard_map.59), kind=kLoop, calls=%fused_computation | loop fusion | bytes 4194304 | tf_op jit(solution)/shard_map/squeeze | solution.py:416

commit v7 on v6

--- a/solution.py
+++ b/solution.py
@@ -275,14 +275,20 @@
     project_all(WINDOW, rows, 0)
     pl.when(has_left)(lambda: to_right().wait_recv())
     pl.when(has_right)(lambda: to_left().wait_recv())
-    for chunk in range(chunks):
-        cross(chunk).start()
+    middle = mid_low | mid_high
+
+    def start_cross():
+        for chunk in range(chunks):
+            cross(chunk).start()
+
+    pl.when(jnp.logical_not(middle))(start_cross)
     normalise(x_halo, 0, 0, 0, WINDOW)
     normalise(x_halo, 0, WINDOW, WINDOW + rows, WINDOW)
     for end, size in ends:
         project_all(end, size, tiles)
 
     def fwd_step(pair, carry):
+        pl.when(middle & (pair == pairs - 1))(start_cross)
         attend(0, pair)
         return carry
 
@@ -292,9 +298,8 @@
     outer = jnp.where(me < count // 2, 1, 0)
     inner = 1 - outer
     outer_start, inner_start = outer * (WINDOW + rows), inner * (WINDOW + rows)
-    middle = mid_low | mid_high
     edge = no_left | no_right
-    early = ((me < count // 4) | (me >= count - count // 4)) & jnp.logical_not(edge)
+    early = jnp.logical_not(edge | middle)
 
     pl.when(mid_low)(lambda: keep_low.wait())
     pl.when(mid_high)(lambda: keep_high.wait())

time: 117 us -> 117 us (level)
  no operation moved by 1% of the time
where the time goes in v7:
time: 117 us
  Pallas kernels  113 us (97%)
  local copies, waits for them, and re-layouts  3.03 us (3%)
    pallas_call x1, Pallas kernels, per_device(): pl.pallas_call(functools.partial(kernel, count, scale), in_specs=[inside,...  113 us
    squeeze x1, local copies, waits for them, and re-layouts, per_device(): return (y[0], y[1])  3.03 us

profile of v7, /device:TPU:12, one launch (start us, length us, event | category | flops | bytes accessed | tf_op | source)
XLA Modules:
  0.0 116.9 jit_solution(2318910667281224410)
XLA Ops:
  0.6 113.2 %shard_map.59 = bf16[2,512,1024]{2,1,0:T(8,128)(2,1)} custom-call(bf16[1024]{0:T(1024)(128)(2,1)} %gain_ref.1, bf16[512,1024]{1,0:T(8,128)(2,1)} %xf_ref.1, bf16[512,1024]{1,0:T(8,128)(2,1)} %xr_ref.1, bf16[1024,3072]{1,0:T(8,128)(2,1)} %w_ref.1), custom_call_target="tpu_custom_call" | custom-call | flops 12884901888 | bytes 10485760 | tf_op jit(solution)/shard_map/pallas_call | solution.py:385
  113.8 3.0 %slice_bitcast_fusion = (bf16[512,1024]{1,0:T(8,128)(2,1)}, bf16[512,1024]{1,0:T(8,128)(2,1)}) fusion(bf16[2,512,1024]{2,1,0:T(8,128)(2,1)} %shard_map.59), kind=kLoop, calls=%fused_computation | loop fusion | bytes 4194304 | tf_op jit(solution)/shard_map/squeeze | solution.py:421
